TPU v7x, 1024 devices: a whole 8x8x8 slice. The times are simulated.
1024 devices in a mesh: lat: 16 (over x_hi, y), lon: 8 (over z), fsdp: 8 (over x_lo, core).
Axes of the slice: x: 8 (x_hi: 2, x_lo: 4; x = x_hi * 4 + x_lo), y: 8, z: 8, core: 2. Of those that a mesh axis runs over, the one named last changes fastest.
Arguments:
- latent: bfloat16 [8, 2, 96, 96, 512], P('fsdp', None, 'lat', 'lon'), may hold values from -6 to 6
- norm_gain: float32 [2, 512], replicated, may hold values from 0.1 to 1.9
- qkv_weight: bfloat16 [2, 512, 1536], P(None, 'fsdp'), may hold values from -0.25 to 0.25
- out_weight: bfloat16 [2, 512, 512], P(None, 'fsdp'), may hold values from -0.25 to 0.25
- rel_bias: float32 [2, 759, 16], replicated, may hold values from -4 to 304, as said below
- bias_index: int32 [144, 144], replicated, may hold values from 0 to 758
- region_ids: int32 [2, 96, 96], P(None, 'lat', 'lon'), may hold values from 0 to 3
Outputs:
- mixed: bfloat16 [8, 2, 96, 96, 512], P('fsdp', None, 'lat', 'lon')
Inputs may be any that keep to these rules, and one draw needn't show every extreme that they name: `rel_bias`: in the hidden draw.
All inputs are finite; a program needn't handle non-finite values.
Results may differ from a plain program's by a relative error of at most 0.012.
Values may be sent and summed in bfloat16 or wider, within the bound.
A program may use at most 64 MiB of HBM per device.

v0:
```python
import jax
import jax.numpy as jnp
from jax import lax
from jax.sharding import PartitionSpec as P

D = 512
HEADS = 16
HEAD_DIM = 32
WZ = 2
WH = 6
WW = 12
WIN = 144


def passed_along(block, axis, distance):
    devices = range(lax.axis_size(axis))
    route = [((i - distance) % len(devices), i) for i in devices]
    return lax.ppermute(block, axis, route)


def layer_norm(hidden, gain_row):
    values = hidden.astype(jnp.float32)
    centre = jnp.mean(values, axis=-1, keepdims=True)
    shifted = values - centre
    variance = jnp.mean(shifted * shifted, axis=-1, keepdims=True)
    return (shifted * lax.rsqrt(variance + 1e-05) * gain_row).astype(jnp.bfloat16)


def bias_table(rel_bias, bias_index, block_index):
    return jnp.take(jnp.transpose(rel_bias[block_index]), bias_index, axis=1)


def split_tile(field_tile):
    sample_count, level_count, row_count, col_count, feature_width = field_tile.shape
    pieces = field_tile.reshape(
        sample_count, level_count // WZ, WZ, row_count // WH, WH, col_count // WW, WW, feature_width
    )
    pieces = jnp.transpose(pieces, (0, 1, 3, 5, 2, 4, 6, 7))
    return pieces.reshape(-1, WIN, feature_width)


def merge_tile(windows, tile_shape):
    sample_count, level_count, row_count, col_count, feature_width = tile_shape
    pieces = windows.reshape(
        sample_count, level_count // WZ, row_count // WH, col_count // WW, WZ, WH, WW, feature_width
    )
    pieces = jnp.transpose(pieces, (0, 1, 4, 2, 5, 3, 6, 7))
    return pieces.reshape(tile_shape)


def attend(normed, weight, bias_heads, region_tags):
    packed = jnp.dot(normed.reshape(-1, D), weight, preferred_element_type=jnp.float32).astype(
        jnp.bfloat16
    )
    packed = split_tile(packed.reshape(normed.shape[:-1] + (3 * D,)))
    packed = packed.reshape(-1, WIN, 3, HEADS, HEAD_DIM)
    scores = jnp.einsum(
        "gqhd,gkhd->ghqk", packed[:, :, 0], packed[:, :, 1], preferred_element_type=jnp.float32
    )
    scores = scores * HEAD_DIM ** (-0.5) + bias_heads[None]
    if region_tags is not None:
        window_tags = split_tile(region_tags[..., None])[..., 0]
        allowed = window_tags[:, :, None] == window_tags[:, None, :]
        blocked = jnp.where(allowed, jnp.float32(0.0), -jnp.inf)
        scores = scores + blocked[:, None]
    row_peak = jnp.max(scores, axis=-1, keepdims=True)
    exponent = jnp.exp(scores - row_peak)
    row_total = jnp.sum(exponent, axis=-1, keepdims=True)
    attn_probs = (exponent / row_total).astype(jnp.bfloat16)
    mixed_out = jnp.einsum(
        "ghqk,gkhd->gqhd", attn_probs, packed[:, :, 2], preferred_element_type=jnp.float32
    )
    return merge_tile(mixed_out.astype(jnp.bfloat16).reshape(-1, WIN, D), normed.shape)


def local(latent, norm_gain, qkv_weight, out_weight, rel_bias, bias_index, region_ids):
    half_rows = WH // 2
    half_cols = WW // 2
    row_count = latent.shape[2]
    col_count = latent.shape[3]

    def fetch_weights(block_index):
        return (
            lax.all_gather(qkv_weight[block_index], "fsdp", axis=0, tiled=True),
            lax.all_gather(out_weight[block_index], "fsdp", axis=0, tiled=True),
        )

    first_qkv, first_out = fetch_weights(0)
    normed = layer_norm(latent, norm_gain[0])
    mixed_out = attend(normed, first_qkv, bias_table(rel_bias, bias_index, 0), None)
    projected = jnp.dot(mixed_out.reshape(-1, D), first_out, preferred_element_type=jnp.float32)
    middle = (latent.astype(jnp.float32) + projected.reshape(latent.shape)).astype(jnp.bfloat16)
    second_qkv, second_out = fetch_weights(1)
    normed = jnp.roll(layer_norm(middle, norm_gain[1]), -1, axis=1)
    east_strip = passed_along(normed[:, :, :, :half_cols], "lon", -1)
    widened = jnp.concatenate([normed[:, :, :, half_cols:], east_strip], axis=3)
    north_strip = passed_along(widened[:, :, :half_rows], "lat", -1)
    rolled = jnp.concatenate([widened[:, :, half_rows:], north_strip], axis=2)
    level_pos = lax.broadcasted_iota(jnp.int32, region_ids.shape, 0)
    row_pos = (
        lax.broadcasted_iota(jnp.int32, region_ids.shape, 1) + lax.axis_index("lat") * row_count
    )
    region_tags = region_ids * 4 + (level_pos == region_ids.shape[0] - 1).astype(jnp.int32) * 2
    region_tags = region_tags + (row_pos >= row_count * lax.axis_size("lat") - half_rows).astype(
        jnp.int32
    )
    region_tags = region_tags[None]
    mixed_out = attend(rolled, second_qkv, bias_table(rel_bias, bias_index, 1), region_tags)
    south_strip = passed_along(mixed_out[:, :, row_count - half_rows :], "lat", 1)
    widened = jnp.concatenate([south_strip, mixed_out[:, :, : row_count - half_rows]], axis=2)
    west_strip = passed_along(widened[:, :, :, col_count - half_cols :], "lon", 1)
    mixed_out = jnp.concatenate([west_strip, widened[:, :, :, : col_count - half_cols]], axis=3)
    mixed_out = jnp.roll(mixed_out, 1, axis=1)
    projected = jnp.dot(mixed_out.reshape(-1, D), second_out, preferred_element_type=jnp.float32)
    return (middle.astype(jnp.float32) + projected.reshape(latent.shape)).astype(jnp.bfloat16)


def solution(mesh):
    return jax.shard_map(
        local,
        mesh=mesh,
        in_specs=(
            P("fsdp", None, "lat", "lon", None),
            P(),
            P(None, "fsdp", None),
            P(None, "fsdp", None),
            P(),
            P(),
            P(None, "lat", "lon"),
        ),
        out_specs=P("fsdp", None, "lat", "lon", None),
        check_vma=False,
    )
```

profile of v0, /device:TPU:1, one launch (start us, length us, event | category | flops | bytes accessed | tf_op | source)
XLA Modules:
  0.0 226.7 jit_solution(11808419018450261304)
XLA Ops:
  6.5 1.8 fusion.28
  11.0 1.5 fusion.33
  12.8 38.7 %gather_fusion = f32[20736,16]{1,0:T(8,128)} fusion(f32[16,759]{0,1:T(8,128)S(1)} %bitcast.94, s32[21504]{0:T(1024)S(1)} %pad_clamp_fusion), kind=kCustom, calls=%fused_computation.clone | custom fusion | bytes 2737152 | tf_op jit(solution)/shard_map/jit(_take)/gather | solution.py:30
  51.5 11.7 %copy.30 = f32[144,144,16]{0,1,2:T(8,128)S(1)} copy(f32[144,144,16]{2,1,0:T(8,128)} %bitcast.97) | data formatting | bytes 2654208 | tf_op jit(solution)/shard_map/jit(_take)/gather | solution.py:30
  64.5 29.3 %all-gather.1 = bf16[1,512,512]{2,1,0:T(8,128)(2,1)S(1)} all-gather(bf16[1,64,512]{2,1,0:T(8,128)(2,1)S(1)} %get-tuple-element.19), channel_id=3, replica_groups=mesh['lat'=16,'lon'=8,'fsdp'=8] {'fsdp'}, dimensions={1}, use_global_device_ids=true | all-gather | bytes 589824 | tf_op jit(solution)/shard_map/all_gather | solution.py:85
  93.8 2.6 %convolution_convert_fusion.1 = bf16[144,1536]{1,0:T(8,128)(2,1)} fusion(bf16[144,512]{1,0:T(8,128)(2,1)S(1)} %reshape.193, bf16[1,512,1536]{2,1,0:T(8,128)(2,1)} %all-gather.7.cloned.1.call-done), kind=kOutput, calls=%fused_computation.5 | convolution fusion | flops 226713600 | bytes 2162688 | tf_op jit(solution)/shard_map/dot_general | solution.py:52
  96.4 2.2 copy.26
  98.6 1.6 bitcast_add_fusion.1
  100.2 1.4 copy-done.1
  102.0 3.1 %fusion.10 = bf16[1,144,16,32]{1,3,2,0:T(8,128)(2,1)S(1)} fusion(f32[16,144]{1,0:T(8,128)S(1)} %fusion.35, bf16[1,144,3,16,32]{1,4,3,2,0:T(8,128)(2,1)} %bitcast.101, f32[16,144,144]{1,2,0:T(8,128)} %copy-done.1), kind=kOutput, calls=%fused_computation.24 | convolution fusion | flops 22305168 | bytes 5137408 | tf_op jit(solution)/shard_map/ghqk,gkhd->gqhd/dot_general | solution.py:70
  107.0 4.8 %collective-permute-start = (bf16[1,2,6,6,512]{4,3,2,1,0:T(8,128)(2,1)S(1)}, bf16[1,2,6,6,512]{4,3,2,1,0:T(8,128)(2,1)S(1)}, u32[]{:S(2)}, u32[]{:S(2)}) collective-permute-start(bf16[1,2,6,6,512]{4,3,2,1,0:T(8,128)(2,1)S(1)} %get-tuple-element.15), channel_id=1, source_target_pairs={{8,0},{16,8},{24,16},{32,24},{40,32},{48,40},{56,48},{0,56},{9,1},... | collective-permute-start | bytes 221192 | tf_op jit(solution)/shard_map/ppermute | solution.py:18
  112.0 1.8 collective-permute-done
  113.9 10.6 %collective-permute-start.1 = (bf16[1,2,3,12,512]{4,3,2,1,0:T(8,128)(2,1)S(1)}, bf16[1,2,3,12,512]{4,3,2,1,0:T(8,128)(2,1)S(1)}, u32[]{:S(2)}, u32[]{:S(2)}) collective-permute-start(bf16[1,2,3,12,512]{4,3,2,1,0:T(8,128)(2,1)S(1)} %get-tuple-element.13), channel_id=1, source_target_pairs={{64,0},{128,64},{192,128},{256,192},{320,256},{384,320},{448,384},... | collective-permute-start | bytes 221192 | tf_op jit(solution)/shard_map/ppermute | solution.py:18
  125.4 38.7 %gather_fusion.1 = f32[20736,16]{1,0:T(8,128)} fusion(f32[16,759]{0,1:T(8,128)S(1)} %bitcast.95, s32[21504]{0:T(1024)S(1)} %pad_clamp_fusion), kind=kCustom, calls=%fused_computation.1.clone | custom fusion | bytes 2737152 | tf_op jit(solution)/shard_map/jit(_take)/gather | solution.py:30
  164.1 11.7 %copy.37 = f32[144,144,16]{0,1,2:T(8,128)S(1)} copy(f32[144,144,16]{2,1,0:T(8,128)} %bitcast.96) | data formatting | bytes 2654208 | tf_op jit(solution)/shard_map/jit(_take)/gather | solution.py:30
  175.9 2.6 %convolution_convert_fusion = bf16[144,1536]{1,0:T(8,128)(2,1)} fusion(bf16[144,512]{1,0:T(8,128)(2,1)S(1)} %reshape.198, bf16[1,512,1536]{2,1,0:T(8,128)(2,1)} %all-gather.9.cloned.1.call-done), kind=kOutput, calls=%fused_computation.4 | convolution fusion | flops 226713600 | bytes 2162688 | tf_op jit(solution)/shard_map/dot_general | solution.py:52
  178.4 1.3 copy.33
  179.7 1.5 fusion.2
  181.3 1.4 copy-done
  183.2 3.0 %fusion.11 = bf16[1,144,16,32]{1,3,2,0:T(8,128)(2,1)S(1)} fusion(f32[16,144]{1,0:T(8,128)S(1)} %fusion.37, bf16[1,144,3,16,32]{1,4,3,2,0:T(8,128)(2,1)S(1)} %bitcast.99, f32[16,144,144]{1,2,0:T(8,128)} %copy-done), kind=kOutput, calls=%fused_computation.25 | convolution fusion | flops 22305168 | bytes 5144576 | tf_op jit(solution)/shard_map/ghqk,gkhd->gqhd/dot_general | solution.py:70
  187.3 1.9 collective-permute-start.2
  189.2 9.7 %collective-permute-done.2 = bf16[1,2,3,12,512]{4,3,2,1,0:T(8,128)(2,1)S(1)} collective-permute-done((bf16[1,2,3,12,512]{4,3,2,1,0:T(8,128)(2,1)S(1)}, bf16[1,2,3,12,512]{4,3,2,1,0:T(8,128)(2,1)S(1)}, u32[]{:S(2)}, u32[]{:S(2)}) %collective-permute-start.2) | collective-permute-done | bytes 73760 | tf_op jit(solution)/shard_map/ppermute | solution.py:18
  199.0 1.9 collective-permute-start.3
  200.9 17.7 %all-gather.3 = bf16[1,512,512]{2,1,0:T(8,128)(2,1)S(1)} all-gather(bf16[1,64,512]{2,1,0:T(8,128)(2,1)S(1)} %copy-done.4), channel_id=5, replica_groups=mesh['lat'=16,'lon'=8,'fsdp'=8] {'fsdp'}, dimensions={1}, use_global_device_ids=true | all-gather | bytes 589824 | tf_op jit(solution)/shard_map/all_gather | solution.py:85
  (67 shorter events, 10.4 us)
Async XLA Ops:
  6.5 87.3 %all-gather.7.cloned.1.call-start = ((), (), s32[]{:S(2)}) async-start(), calls=%async_computation | async-start | bytes 1769472 | tf_op jit(solution)/shard_map/all_gather | solution.py:84
  8.3 167.5 %all-gather.9.cloned.1.call-start = ((), (), s32[]{:S(2)}) async-start(), calls=%async_computation.1 | async-start | bytes 1769472 | tf_op jit(solution)/shard_map/all_gather | solution.py:84
  51.4 11.9 %copy-start.8 = (f32[2,512]{1,0:T(2,128)S(1)}, f32[2,512]{1,0:T(2,128)}, u32[]{:S(2)}) copy-start(f32[2,512]{1,0:T(2,128)} %param.10) | copy-start | bytes 12292
  51.5 11.9 %copy-start.2 = (bf16[1,2,6,12,512]{4,1,3,2,0:T(2,128)(2,1)S(1)}, bf16[1,2,6,12,512]{4,1,3,2,0:T(2,128)(2,1)}, u32[]{:S(2)}) copy-start(bf16[1,2,6,12,512]{4,1,3,2,0:T(2,128)(2,1)} %param.9) | copy-start | bytes 442372
  51.5 12.4 %copy-start.6 = (bf16[2,64,512]{2,1,0:T(8,128)(2,1)S(1)}, bf16[2,64,512]{2,1,0:T(8,128)(2,1)}, u32[]{:S(2)}) copy-start(bf16[2,64,512]{2,1,0:T(8,128)(2,1)} %param.12) | copy-start | bytes 393220
  63.3 35.2 %copy-start.3 = (pred[144,144]{0,1:T(8,128)(4,1)}, pred[144,144]{0,1:T(8,128)(4,1)S(1)}, u32[]{:S(2)}) copy-start(pred[144,144]{0,1:T(8,128)(4,1)S(1)} %copy.27) | copy-start | bytes 62212
  100.1 1.4 copy-start.1
  105.2 6.7 %copy-start.7 = (s32[2,6,12]{2,0,1:T(2,128)S(1)}, s32[2,6,12]{2,0,1:T(2,128)}, u32[]{:S(2)}) copy-start(s32[2,6,12]{2,0,1:T(2,128)} %param.15) | copy-start | bytes 1732
  105.7 19.6 %copy-start.5 = (f32[1,759,16]{1,2,0:T(8,128)S(1)}, f32[1,759,16]{1,2,0:T(8,128)}, u32[]{:S(2)}) copy-start(f32[1,759,16]{1,2,0:T(8,128)} %get-tuple-element.20) | copy-start | bytes 145732
  107.0 6.8 %collective-permute-start = (bf16[1,2,6,6,512]{4,3,2,1,0:T(8,128)(2,1)S(1)}, bf16[1,2,6,6,512]{4,3,2,1,0:T(8,128)(2,1)S(1)}, u32[]{:S(2)}, u32[]{:S(2)}) collective-permute-start(bf16[1,2,6,6,512]{4,3,2,1,0:T(8,128)(2,1)S(1)} %get-tuple-element.15), channel_id=1, source_target_pairs={{8,0},{16,8},{24,16},{32,24},{40,32},{48,40},{56,48},{0,56},{9,1},... | collective-permute-start | bytes 221192 | tf_op jit(solution)/shard_map/ppermute | solution.py:18
  113.9 61.8 %collective-permute-start.1 = (bf16[1,2,3,12,512]{4,3,2,1,0:T(8,128)(2,1)S(1)}, bf16[1,2,3,12,512]{4,3,2,1,0:T(8,128)(2,1)S(1)}, u32[]{:S(2)}, u32[]{:S(2)}) collective-permute-start(bf16[1,2,3,12,512]{4,3,2,1,0:T(8,128)(2,1)S(1)} %get-tuple-element.13), channel_id=1, source_target_pairs={{64,0},{128,64},{192,128},{256,192},{320,256},{384,320},{448,384},... | collective-permute-start | bytes 221192 | tf_op jit(solution)/shard_map/ppermute | solution.py:18
  181.3 1.4 copy-start
  186.2 14.7 %copy-start.4 = (bf16[1,64,512]{2,1,0:T(8,128)(2,1)S(1)}, bf16[1,64,512]{2,1,0:T(8,128)(2,1)}, u32[]{:S(2)}) copy-start(bf16[1,64,512]{2,1,0:T(8,128)(2,1)} %get-tuple-element.18) | copy-start | bytes 196612
  187.3 11.7 %collective-permute-start.2 = (bf16[1,2,3,12,512]{4,3,2,1,0:T(8,128)(2,1)S(1)}, bf16[1,2,3,12,512]{4,3,2,1,0:T(8,128)(2,1)S(1)}, u32[]{:S(2)}, u32[]{:S(2)}) collective-permute-start(bf16[1,2,3,12,512]{4,3,2,1,0:T(8,128)(2,1)S(1)} %get-tuple-element.10), channel_id=1, source_target_pairs={{960,0},{0,64},{64,128},{128,192},{192,256},{256,320},{320,384},{3... | collective-permute-start | bytes 221192 | tf_op jit(solution)/shard_map/ppermute | solution.py:18
  199.0 19.7 %collective-permute-start.3 = (bf16[1,2,6,6,512]{4,3,2,1,0:T(8,128)(2,1)S(1)}, bf16[1,2,6,6,512]{4,3,2,1,0:T(8,128)(2,1)S(1)}, u32[]{:S(2)}, u32[]{:S(2)}) collective-permute-start(bf16[1,2,6,6,512]{4,3,2,1,0:T(8,128)(2,1)S(1)} %fusion.22), channel_id=1, source_target_pairs={{56,0},{0,8},{8,16},{16,24},{24,32},{32,40},{40,48},{48,56},{57,1}... | collective-permute-start | bytes 221192 | tf_op jit(solution)/shard_map/ppermute | solution.py:18
Sparse Core Ops, SparseCore 0:
  10.0 54.7 all-gather.6
  67.5 43.2 all-gather.8
where the time goes:
time: 227 us
  local copies, waits for them, and re-layouts  114 us (50%)
  blocking collectives  47 us (21%)
  starting transfers between devices  19.3 us (9%)
  matrix products  15 us (7%)
  between operations  13.8 us (6%)
  waiting for transfers between devices  12.3 us (5%)
  other arithmetic  4.74 us (2%)
    gather x4, local copies, waits for them, and re-layouts, bias_table(): return jnp.take(jnp.transpose(rel_bias[block_index]), bias_index, axis=1)  101 us
    all_gather x2, blocking collectives, fetch_weights(): lax.all_gather(out_weight[block_index], 'fsdp', axis=0, tiled=True)  47 us
    ppermute x4, starting transfers between devices, passed_along(): return lax.ppermute(block, axis, route)  19.2 us
    ppermute x4, waiting for transfers between devices, passed_along(): return lax.ppermute(block, axis, route)  11.6 us
    dot_general x2, matrix products, attend(): jnp.einsum('ghqk,gkhd->gqhd', attn_probs, packed[:, :, 2], preferred_elem...  6.18 us
    dot_general x2, matrix products, attend(): jnp.dot(normed.reshape(-1, D), weight, preferred_element_type=jnp.float32)  5.17 us
  transfers between devices with their start and end apart: 6, of which 2 were waited for; matrix products, arithmetic and copies ran while one was open for 52% of the time, Pallas kernels for 0%

commit v1 on v0

v1 whole, which is shorter than its diff:
```python
import functools

import jax
import jax.numpy as jnp
import numpy as np
from jax import lax
from jax.experimental import pallas as pl
from jax.experimental.pallas import tpu as pltpu
from jax.sharding import PartitionSpec as P

D = 512
HEADS = 16
HEAD_DIM = 32
WZ = 2
WH = 6
WW = 12
WIN = 144
HH = WH // 2
HW = WW // 2
QUAD = WZ * HH * HW
QPAD = 48
SPAD = 80
ROWS = WIN + 6 * SPAD
BIAS_ROWS = 759
LOG2E = 1.4426950408889634
SCALE = LOG2E * HEAD_DIM ** (-0.5)
BLOCKED = -1e30
MESH = pl.DeviceIdType.MESH
F32 = jnp.float32
BF16 = jnp.bfloat16


def token(z, h, w):
    return (z * WH + h) * WW + w


def one_hot_rows(sources, row_count, width):
    table = np.zeros((row_count, width), np.float32)
    for row, source in enumerate(sources):
        if source >= 0:
            table[row, source] = 1.0
    return table.astype(jnp.bfloat16)


@functools.cache
def selections():
    tokens = [(z, h, w) for z in range(WZ) for h in range(WH) for w in range(WW)]
    pad = [-1] * (SPAD - WIN // 2)
    north = [token(*t) for t in tokens if t[1] < HH] + pad
    south = [token(*t) for t in tokens if t[1] >= HH] + pad
    west = [token(*t) for t in tokens if t[2] < HW] + pad
    east = [token(*t) for t in tokens if t[2] >= HW] + pad
    strips = one_hot_rows(north + south + west + east, 4 * SPAD, WIN)

    def corner(first):
        rows = []
        for side in range(2):
            for z in range(WZ):
                for h in range(HH):
                    for w in range(HW):
                        rows.append(side * SPAD + (z * HH + h) * WW + first + w)
        return rows + pad

    corners = one_hot_rows(corner(0) + corner(HW), 2 * SPAD, 2 * SPAD)

    def source(z, row, col):
        n, s, w_, e, cw, ce = (WIN + k * SPAD for k in range(6))
        if HH <= row < HH + WH:
            h = row - HH
            if col < HW:
                return w_ + (z * WH + h) * HW + col
            if col < HW + WW:
                return token(z, h, col - HW)
            return e + (z * WH + h) * HW + col - HW - WW
        side = 0 if row < HH else 1
        h = row if row < HH else row - HH - WH
        if col < HW:
            return cw + side * QUAD + (z * HH + h) * HW + col
        if col < HW + WW:
            return (n, s)[side] + (z * HH + h) * WW + col - HW
        return ce + side * QUAD + (z * HH + h) * HW + col - HW - WW

    keys = []
    query_token = []
    query_place = []
    for a in range(2):
        for b in range(2):
            for dz, dh, dw in tokens:
                keys.append(source((dz + 1) % WZ, a * WH + dh, b * WW + dw))
            for z in range(WZ):
                for h in range(a * HH, a * HH + HH):
                    for w in range(b * HW, b * HW + HW):
                        query_token.append(token(z, h, w))
                        query_place.append(token((z - 1) % WZ, (h - HH) % WH, (w - HW) % WW))
            query_token += [-1] * (QPAD - QUAD)
            query_place += [-1] * (QPAD - QUAD)
    key_rows = one_hot_rows(keys, 4 * WIN, ROWS)
    query_rows = one_hot_rows(query_token, 4 * QPAD, WIN)
    place_rows = one_hot_rows(query_place, 4 * QPAD, 256)
    places = np.full((8, 256), -1, np.int32)
    for j, (dz, dh, dw) in enumerate(tokens):
        places[0, j] = dh * WZ + dz
        places[1, j] = dw
        places[2, j] = dz
        places[3, j] = dh
    return strips, corners, key_rows, query_rows, np.ascontiguousarray(query_rows.T), place_rows, places


def normalize(values, gain_row):
    centre = jnp.mean(values, axis=-1, keepdims=True)
    shifted = values - centre
    variance = jnp.mean(shifted * shifted, axis=-1, keepdims=True)
    return (shifted * lax.rsqrt(variance + 1e-05) * gain_row).astype(BF16)


def picked(table, places):
    return jnp.take_along_axis(table, places, axis=1, mode="promise_in_bounds")


def kernel(
    x_ref, gain_ref, qkv_ref, outw_ref, table_ref, idx_ref, region_ref,
    strip_ref, corner_ref, key_ref, query_ref, back_ref, place_ref, pos_ref,
    out_ref,
    wq, wo, table, index, index_out, regions, tags, allowed,
    bias0, bias1, normed, qkv0, mixed0, middle, rows, strip_out, corner_out, xq, xk, q1, kv1, mixed1,
    local_sem, send_sem, recv_sem,
    *, lat_count, lon_count,
):
    la, lo, fs = lax.axis_index("lat"), lax.axis_index("lon"), lax.axis_index("fsdp")
    y_count = lat_count // 2
    y, core, x = la % y_count, fs % 2, (la // y_count) * 4 + fs // 2

    def along_x(step):
        there = (x + step) % 8
        return ((there // 4) * y_count + y, lo, (there % 4) * 2 + core)

    right, left = along_x(1), along_x(7)
    sibling = (la, lo, fs + 1 - 2 * core)
    north = ((la + lat_count - 1) % lat_count, lo, fs)
    south = ((la + 1) % lat_count, lo, fs)
    west = (la, (lo + lon_count - 1) % lon_count, fs)
    east = (la, (lo + 1) % lon_count, fs)
    partners = (right, left, sibling, north, south, west, east)
    barrier = pltpu.get_barrier_semaphore()
    for partner in partners:
        pl.semaphore_signal(barrier, inc=1, device_id=partner, device_id_type=MESH)

    counter = [0]
    sent = []

    def send(source, target, device):
        copy = pltpu.make_async_remote_copy(
            src_ref=source, dst_ref=target, send_sem=send_sem.at[counter[0]], recv_sem=recv_sem.at[counter[0]],
            device_id=device, device_id_type=MESH,
        )
        counter[0] += 1
        copy.start()
        sent.append(copy)
        return copy

    shard = D // 8
    half = shard // 2
    weights = {0: (wq.at[0], qkv_ref.at[0]), 1: (wo.at[0], outw_ref.at[0]), 2: (wq.at[1], qkv_ref.at[1]), 3: (wo.at[1], outw_ref.at[1])}
    own_row = fs * shard
    from_right = right[2] * shard
    from_left = left[2] * shard
    across = ((fs + 4) % 8) * shard

    def part(ref, start, size):
        return ref.at[pl.ds(pl.multiple_of(start, half), size)]

    held = []
    for k in range(4):
        full, mine = weights[k]
        copy = pltpu.make_async_copy(mine, part(full, own_row, shard), local_sem.at[k])
        copy.start()
        held.append(copy)

    table[...] = jnp.zeros_like(table)
    table[:, :, :BIAS_ROWS] = table_ref[...] * LOG2E
    index[...] = jnp.zeros_like(index)
    index[:, :WIN] = idx_ref[...]
    pl.semaphore_wait(barrier, len(partners))

    stages = {}

    def start_weights(k):
        full, mine = weights[k]
        to_left = send(mine.at[pl.ds(0, half)], part(full, own_row, half), left)
        to_right = send(mine.at[pl.ds(half, half)], part(full, own_row + half, half), right)
        to_left2 = send(mine.at[pl.ds(half, half)], part(full, own_row + half, half), left)
        to_right2 = send(mine.at[pl.ds(0, half)], part(full, own_row, half), right)
        to_sibling = send(mine, part(full, own_row, shard), sibling)
        stages[k] = [to_left, to_right, to_left2, to_right2, to_sibling]

    def pass_first(k):
        full, _ = weights[k]
        first, second = stages[k][0], stages[k][1]
        first.wait_recv()
        low = part(full, from_right, half)
        relay_left = send(low, low, left)
        share_low = send(low, low, sibling)
        second.wait_recv()
        high = part(full, from_left + half, half)
        relay_right = send(high, high, right)
        share_high = send(high, high, sibling)
        stages[k] += [relay_left, relay_right, share_low, share_high]

    def pass_second(k):
        full, _ = weights[k]
        stages[k][2].wait_recv()
        high = part(full, from_right + half, half)
        share_high = send(high, high, sibling)
        stages[k][3].wait_recv()
        low = part(full, from_left, half)
        share_low = send(low, low, sibling)
        stages[k] += [share_high, share_low]

    def pass_across(k):
        full, _ = weights[k]
        stages[k][5].wait_recv()
        low = part(full, across, half)
        share_low = send(low, low, sibling)
        stages[k][6].wait_recv()
        high = part(full, across + half, half)
        share_high = send(high, high, sibling)
        stages[k] += [share_low, share_high]

    def finish_weights(k):
        held[k].wait()
        for at in (4, 7, 8, 9, 10, 11, 12):
            stages[k][at].wait_recv()

    start_weights(0)

    region_rows = jnp.zeros((16, 128), F32)
    regions[...] = region_rows
    for h in range(WH):
        regions[WZ * h : WZ * h + WZ, :WW] = region_ref[h].astype(F32)
    pos = pos_ref[...]
    row_hot = (lax.broadcasted_iota(jnp.int32, (16, 256), 0) == pos[0:1]).astype(F32)
    spread = lax.dot_general(regions[...], row_hot, (((0,), (0,)), ((), ())), preferred_element_type=F32)
    col_hot = lax.broadcasted_iota(jnp.int32, (128, 256), 0) == pos[1:2]
    region_row = jnp.sum(jnp.where(col_hot, spread, 0.0), axis=0, keepdims=True)
    last_rows = jnp.where(la == lat_count - 1, 1.0, 0.0) * (pos[3:4] >= HH).astype(F32)
    tag_row = region_row * 4.0 + 2.0 * (pos[2:3] == WZ - 1).astype(F32) + last_rows
    tags[3] = jnp.broadcast_to(tag_row, (8, 256))
    tag_south = send(tags.at[3], tags.at[1], south)
    tag_east = send(tags.at[3], tags.at[2], east)

    normed[...] = normalize(x_ref[...].astype(F32), gain_ref[0:1])

    def bias_rows0(first, count):
        @pl.loop(first, first + count)
        def _(r):
            span = pl.ds(pl.multiple_of(r * 8, 8), 8)
            for side in range(2):
                lanes = slice(side * 128, side * 128 + 128)
                places = index[span, lanes]
                lane = places & 127
                chunk = places >> 7
                for h in range(HEADS):
                    total = None
                    for c in range(6):
                        piece = picked(jnp.broadcast_to(table[0, h : h + 1, c * 128 : c * 128 + 128], (8, 128)), lane)
                        total = piece if total is None else jnp.where(chunk == c, piece, total)
                    bias0[h, span, lanes] = total

    def bias_rows1(first, count):
        @pl.loop(first, first + count)
        def _(r):
            span = pl.ds(pl.multiple_of(r * 8, 8), 8)
            window = r // 6
            inner = pl.ds(pl.multiple_of((r % 6) * 8, 8), 8)
            for side in range(2):
                lanes = slice(side * 128, side * 128 + 128)
                places = index_out[span, lanes]
                lane = places & 127
                chunk = places >> 7
                keep = allowed[span, lanes] > 0.5
                for h in range(HEADS):
                    total = None
                    for c in range(6):
                        piece = picked(jnp.broadcast_to(table[1, h : h + 1, c * 128 : c * 128 + 128], (8, 128)), lane)
                        total = piece if total is None else jnp.where(chunk == c, piece, total)
                    bias1[window, h, inner, lanes] = jnp.where(keep, total, BLOCKED)

    bias_rows0(0, 6)
    pass_first(0)
    tag_south.wait_recv()
    tag_corner = send(tags.at[1], tags.at[0], east)
    bias_rows0(6, 6)
    pass_second(0)
    start_weights(1)
    bias_rows0(12, 6)
    pass_across(0)
    finish_weights(0)

    @pl.loop(0, 6)
    def _(t):
        lanes = pl.ds(pl.multiple_of(t * 256, 256), 256)
        qkv0[:, lanes] = jnp.dot(normed[...], wq[0, :, lanes], preferred_element_type=F32).astype(BF16)

    pass_first(1)
    start_weights(2)
    lane_head = lax.broadcasted_iota(jnp.int32, (1, 128), 1) // HEAD_DIM

    @pl.loop(0, 4)
    def _(g):
        def cut(base):
            return qkv0[:, pl.ds(pl.multiple_of(base + g * 128, 128), 128)]

        q, k, v = cut(0), cut(D), cut(2 * D)
        v_ones = jnp.concatenate([v, jnp.ones((WIN, 128), BF16)], axis=1)
        top = jnp.zeros((WIN, 128), F32)
        bottom = jnp.zeros((WIN, 128), F32)
        for u in range(4):
            mine = lane_head == u
            scores = lax.dot_general(jnp.where(mine, q, jnp.zeros_like(q)), k, (((1,), (1,)), ((), ())), preferred_element_type=F32)
            scores = scores * SCALE + bias0[g * 4 + u, :, :WIN]
            peak = jnp.max(scores, axis=1, keepdims=True)
            weight = jnp.exp2(scores - peak).astype(BF16)
            both = jnp.dot(weight, v_ones, preferred_element_type=F32)
            top = jnp.where(mine, both[:, :128], top)
            bottom = jnp.where(mine, both[:, 128:], bottom)
        mixed0[:, pl.ds(pl.multiple_of(g * 128, 128), 128)] = (top / bottom).astype(BF16)

    pass_second(1)
    pass_across(1)
    finish_weights(1)
    projected = jnp.dot(mixed0[...], wo[0], preferred_element_type=F32)
    mid = (x_ref[...].astype(F32) + projected).astype(BF16)
    middle[...] = mid
    rows[0:WIN] = normalize(mid.astype(F32), gain_ref[1:2])
    strip_out[...] = jnp.dot(strip_ref[...], rows[0:WIN], preferred_element_type=F32).astype(BF16)

    def slot(k):
        return rows.at[pl.ds(WIN + k * SPAD, SPAD)]

    to_north = send(strip_out.at[pl.ds(0, SPAD)], slot(1), north)
    to_south = send(strip_out.at[pl.ds(SPAD, SPAD)], slot(0), south)
    to_west = send(strip_out.at[pl.ds(2 * SPAD, SPAD)], slot(3), west)
    to_east = send(strip_out.at[pl.ds(3 * SPAD, SPAD)], slot(2), east)

    pass_first(2)
    xq[...] = jnp.dot(query_ref[...], rows[0:WIN], preferred_element_type=F32).astype(BF16)
    places = index[...]
    index_lane = jnp.dot(place_ref[:, :WIN], (places & 127).astype(F32).astype(BF16), preferred_element_type=F32)
    index_chunk = jnp.dot(place_ref[:, :WIN], (places >> 7).astype(F32).astype(BF16), preferred_element_type=F32)
    index_out[...] = (index_chunk * 128.0 + index_lane).astype(jnp.int32)
    tag_east.wait_recv()
    tag_corner.wait_recv()
    for w in range(4):
        span = slice(w * QPAD, w * QPAD + QPAD)
        query_tags = lax.dot_general(place_ref[span], tags[w].astype(BF16), (((1,), (1,)), ((), ())), preferred_element_type=F32)
        allowed[span] = jnp.where(query_tags[:, 0:1] == tags[w, 0:1], 1.0, 0.0)
    bias_rows1(0, 8)
    pass_second(2)
    start_weights(3)
    bias_rows1(8, 8)
    pass_across(2)
    pass_first(3)
    to_north.wait_recv()
    to_south.wait_recv()
    corner_out[...] = jnp.dot(corner_ref[...], rows[WIN : WIN + 2 * SPAD], preferred_element_type=F32).astype(BF16)
    corner_west = send(corner_out.at[pl.ds(0, SPAD)], slot(5), west)
    corner_east = send(corner_out.at[pl.ds(SPAD, SPAD)], slot(4), east)
    bias_rows1(16, 8)
    pass_second(3)
    finish_weights(2)

    @pl.loop(0, 2)
    def _(t):
        lanes = pl.ds(pl.multiple_of(t * 256, 256), 256)
        q1[:, lanes] = jnp.dot(xq[...], wq[1, :, lanes], preferred_element_type=F32).astype(BF16)

    pass_across(3)
    to_west.wait_recv()
    to_east.wait_recv()
    corner_west.wait_recv()
    corner_east.wait_recv()

    @pl.loop(0, 4)
    def _(t):
        span = pl.ds(pl.multiple_of(t * WIN, 16), WIN)
        xk[span] = jnp.dot(key_ref[span], rows[...], preferred_element_type=F32).astype(BF16)

    @pl.loop(0, 4)
    def _(t):
        lanes = pl.ds(pl.multiple_of(t * 256, 256), 256)
        source = pl.ds(pl.multiple_of(D + t * 256, 256), 256)
        kv1[:, lanes] = jnp.dot(xk[...], wq[1, :, source], preferred_element_type=F32).astype(BF16)

    @pl.loop(0, 4)
    def _(g):
        for w in range(4):
            span = slice(w * QPAD, w * QPAD + QPAD)
            keys = slice(w * WIN, w * WIN + WIN)
            q = q1[span, pl.ds(pl.multiple_of(g * 128, 128), 128)]
            k = kv1[keys, pl.ds(pl.multiple_of(g * 128, 128), 128)]
            v = kv1[keys, pl.ds(pl.multiple_of(D + g * 128, 128), 128)]
            v_ones = jnp.concatenate([v, jnp.ones((WIN, 128), BF16)], axis=1)
            stacked = jnp.concatenate([jnp.where(lane_head == u, q, jnp.zeros_like(q)) for u in range(4)], axis=0)
            scores = lax.dot_general(stacked, k, (((1,), (1,)), ((), ())), preferred_element_type=F32)
            bias = bias1[w, pl.ds(g * 4, 4), :, :WIN].reshape(4 * QPAD, WIN)
            scores = scores * SCALE + bias
            peak = jnp.max(scores, axis=1, keepdims=True)
            weight = jnp.exp2(scores - peak).astype(BF16)
            both = jnp.dot(weight, v_ones, preferred_element_type=F32)
            top, bottom = both[:QPAD, :128], both[:QPAD, 128:]
            for u in range(1, 4):
                mine = lane_head == u
                top = jnp.where(mine, both[u * QPAD : u * QPAD + QPAD, :128], top)
                bottom = jnp.where(mine, both[u * QPAD : u * QPAD + QPAD, 128:], bottom)
            mixed1[span, pl.ds(pl.multiple_of(g * 128, 128), 128)] = (top / bottom).astype(BF16)

    finish_weights(3)
    natural = jnp.dot(back_ref[...], mixed1[...], preferred_element_type=F32).astype(BF16)
    projected = jnp.dot(natural, wo[1], preferred_element_type=F32)
    out_ref[...] = (middle[...].astype(F32) + projected).astype(BF16)
    for copy in sent:
        copy.wait_send()


COPIES = 4 * 13 + 3 + 6


def local(lat_count, lon_count, latent, norm_gain, qkv_weight, out_weight, rel_bias, bias_index, region_ids):
    vmem = pl.BlockSpec(memory_space=pltpu.VMEM)
    anywhere = pl.BlockSpec(memory_space=pl.ANY)
    out = pl.pallas_call(
        functools.partial(kernel, lat_count=lat_count, lon_count=lon_count),
        out_shape=jax.ShapeDtypeStruct((WIN, D), BF16),
        in_specs=[vmem, vmem, anywhere, anywhere] + [vmem] * 10,
        out_specs=vmem,
        scratch_shapes=[
            pltpu.VMEM((2, D, 3 * D), BF16),
            pltpu.VMEM((2, D, D), BF16),
            pltpu.VMEM((2, HEADS, 768), F32),
            pltpu.VMEM((WIN, 256), jnp.int32),
            pltpu.VMEM((4 * QPAD, 256), jnp.int32),
            pltpu.VMEM((16, 128), F32),
            pltpu.VMEM((4, 8, 256), F32),
            pltpu.VMEM((4 * QPAD, 256), F32),
            pltpu.VMEM((HEADS, WIN, 256), F32),
            pltpu.VMEM((4, HEADS, QPAD, 256), F32),
            pltpu.VMEM((WIN, D), BF16),
            pltpu.VMEM((WIN, 3 * D), BF16),
            pltpu.VMEM((WIN, D), BF16),
            pltpu.VMEM((WIN, D), BF16),
            pltpu.VMEM((ROWS, D), BF16),
            pltpu.VMEM((4 * SPAD, D), BF16),
            pltpu.VMEM((2 * SPAD, D), BF16),
            pltpu.VMEM((4 * QPAD, D), BF16),
            pltpu.VMEM((4 * WIN, D), BF16),
            pltpu.VMEM((4 * QPAD, D), BF16),
            pltpu.VMEM((4 * WIN, 2 * D), BF16),
            pltpu.VMEM((4 * QPAD, D), BF16),
            pltpu.SemaphoreType.DMA((4,)),
            pltpu.SemaphoreType.DMA((COPIES,)),
            pltpu.SemaphoreType.DMA((COPIES,)),
        ],
        compiler_params=pltpu.CompilerParams(
            collective_id=0, has_side_effects=True, vmem_limit_bytes=48 * 2**20
        ),
        name="two_blocks",
    )(
        latent.reshape(WIN, D), norm_gain, qkv_weight, out_weight,
        jnp.transpose(rel_bias, (0, 2, 1)), bias_index, jnp.transpose(region_ids, (1, 0, 2)),
        *(jnp.asarray(s) for s in selections()),
    )
    return out.reshape(latent.shape)


def solution(mesh):
    return jax.shard_map(
        functools.partial(local, mesh.shape["lat"], mesh.shape["lon"]),
        mesh=mesh,
        in_specs=(
            P("fsdp", None, "lat", "lon", None),
            P(),
            P(None, "fsdp", None),
            P(None, "fsdp", None),
            P(),
            P(),
            P(None, "lat", "lon"),
        ),
        out_specs=P("fsdp", None, "lat", "lon", None),
        check_vma=False,
    )
```

time: 227 us -> 73.4 us (0.32)
  local copies, waits for them, and re-layouts: 114 us -> 10.7 us
  Pallas kernels: 0 us -> 62.2 us
  blocking collectives: 47 us -> 0 us
  starting transfers between devices: 19.3 us -> 0 us
  matrix products: 15 us -> 0 us
  between operations: 13.8 us -> 0.07 us
  waiting for transfers between devices: 12.3 us -> 0 us
  other arithmetic: 4.74 us -> 0 us
    gather x4 -> x0, local copies, waits for them, and re-layouts: 101 us -> none  [bias_table(): return jnp.take(jnp.transpose(rel_bias[block_index]), bias_index, axis=1)]
    pallas_call x0 -> x1, Pallas kernels: none -> 62.2 us  [local(): pl.pallas_call(functools.partial(kernel, lat_count=lat_count, lon_count=l...]
    all_gather x2 -> x0, blocking collectives: 47 us -> none  [fetch_weights(): lax.all_gather(out_weight[block_index], 'fsdp', axis=0, tiled=True)]
    ppermute x4 -> x0, starting transfers between devices: 19.2 us -> none  [passed_along(): return lax.ppermute(block, axis, route)]
    dot_general x8 -> x0, matrix products: 15 us -> none  [the longest x2 6.18 us: attend(): jnp.einsum('ghqk,gkhd->gqhd', attn_probs, packed[:, :, 2], preferred_elem...]
    ppermute x4 -> x0, waiting for transfers between devices: 11.6 us -> none  [passed_along(): return lax.ppermute(block, axis, route)]
    unnamed x20 -> x27, local copies, waits for them, and re-layouts: 3.16 us -> 9.77 us
    convert_element_type x5 -> x0, local copies, waits for them, and re-layouts: 5.24 us -> none  [the longest x2 3.47 us: attend(): jnp.dot(normed.reshape(-1, D), weight, preferred_element_type=jnp.float32)]
  transfers between devices with their start and end apart: 6 -> 0, of which waited for: 2 -> 0; matrix products, arithmetic and copies ran while one was open for 52% -> 0% of each run, Pallas kernels for 0% -> 0%
where the time goes in v1:
time: 73.4 us; the launch traced here: 72.9 us
  Pallas kernels  62.2 us (85%)
  local copies, waits for them, and re-layouts  10.7 us (15%)
    pallas_call x1, Pallas kernels, local(): pl.pallas_call(functools.partial(kernel, lat_count=lat_count, lon_count=l...  62.2 us
    unnamed x27, local copies, waits for them, and re-layouts  9.77 us

profile of v1, /device:TPU:1, one launch (start us, length us, event | category | flops | bytes accessed | tf_op | source)
XLA Modules:
  0.0 72.9 jit_solution(17459947766002726787)
XLA Ops:
  0.0 0.0 copy-start.10
  0.0 0.0 copy-start.1
  0.0 1.0 %copy.17 = bf16[1,2,6,12,512]{4,3,2,1,0:T(8,128)(2,1)S(1)} copy(bf16[1,2,6,12,512]{4,1,3,2,0:T(2,128)(2,1)} %param.14) | data formatting | bytes 294912 | tf_op args[0]
  1.0 0.0 copy-start.2
  1.0 0.0 copy-start.4
  1.1 0.0 copy-done.10
  1.1 0.0 copy-done.1
  1.1 0.8 %copy-done.2 = bf16[320,144]{1,0:T(8,128)(2,1)S(1)} copy-done((bf16[320,144]{1,0:T(8,128)(2,1)S(1)}, bf16[320,144]{1,0:T(8,128)(2,1)}, u32[]{:S(2)}) %copy-start.2) | copy-done | bytes 92184
  1.9 0.1 copy-done.4
  2.0 0.0 copy-start
  2.0 1.1 %copy-done = bf16[576,624]{1,0:T(8,128)(2,1)S(1)} copy-done((bf16[576,624]{1,0:T(8,128)(2,1)S(1)}, bf16[576,624]{1,0:T(8,128)(2,1)}, u32[]{:S(2)}) %copy-start) | copy-done | bytes 718872
  3.1 0.0 copy-start.3
  3.1 0.9 %copy-done.3 = s32[144,144]{1,0:T(8,128)S(1)} copy-done((s32[144,144]{1,0:T(8,128)S(1)}, s32[144,144]{1,0:T(8,128)}, u32[]{:S(2)}) %copy-start.3) | copy-done | bytes 82968
  4.0 0.0 copy-start.5
  4.0 0.9 %copy-done.5 = f32[2,759,16]{1,2,0:T(8,128)S(1)} copy-done((f32[2,759,16]{1,2,0:T(8,128)S(1)}, f32[2,759,16]{1,2,0:T(8,128)}, u32[]{:S(2)}) %copy-start.5) | copy-done | bytes 97176
  4.9 0.0 copy-start.6
  4.9 0.9 %copy-done.6 = bf16[192,256]{1,0:T(8,128)(2,1)S(1)} copy-done((bf16[192,256]{1,0:T(8,128)(2,1)S(1)}, bf16[192,256]{1,0:T(8,128)(2,1)}, u32[]{:S(2)}) %copy-start.6) | copy-done | bytes 98328
  5.8 0.9 %copy-done.7 = bf16[192,144]{1,0:T(8,128)(2,1)S(1)} copy-done((bf16[192,144]{1,0:T(8,128)(2,1)S(1)}, bf16[192,144]{1,0:T(8,128)(2,1)}, u32[]{:S(2)}) %copy-start.7) | copy-done | bytes 55320
  6.7 0.9 %copy-done.8 = bf16[160,160]{1,0:T(8,128)(2,1)S(1)} copy-done((bf16[160,160]{1,0:T(8,128)(2,1)S(1)}, bf16[160,160]{1,0:T(8,128)(2,1)}, u32[]{:S(2)}) %copy-start.8) | copy-done | bytes 51224
  7.6 0.9 %copy-done.9 = bf16[144,192]{1,0:T(8,128)(2,1)S(1)} copy-done((bf16[144,192]{1,0:T(8,128)(2,1)S(1)}, bf16[144,192]{1,0:T(8,128)(2,1)}, u32[]{:S(2)}) %copy-start.9) | copy-done | bytes 55320
  8.5 0.7 copy-done.11
  9.2 0.7 copy-done.12
  9.9 62.2 %two_blocks.1 = bf16[144,512]{1,0:T(8,128)(2,1)S(1)} custom-call(bf16[144,512]{1,0:T(8,128)(2,1)S(1)} %reshape.6.x_ref, f32[2,512]{1,0:T(2,128)S(1)} %copy-done.12, bf16[2,64,1536]{2,1,0:T(8,128)(2,1)S(1)} %copy-done.1, bf16[2,64,512]{2,1,0:T(8,128)(2,1)S(1)} %copy-done.4, f32[2,16,759]{2,1,0:T(8,128)S(1)} %bitcast.2, s32[144,144]{1,0:T(8,128)S(1)} %copy-done.3, ...), custom_call_target="tpu_custom_call" | custom-call | tf_op jit(solution)/shard_map/two_blocks/pallas_call | solution.py:431
  72.1 0.8 %copy.18 = bf16[1,2,6,12,512]{4,1,3,2,0:T(2,128)(2,1)} copy(bf16[1,2,6,12,512]{4,3,2,1,0:T(8,128)(2,1)S(1)} %reshape.7) | data formatting | bytes 294912 | tf_op jit(solution)/shard_map/reshape | solution.py:472
  (7 shorter events, 0.1 us)
Async XLA Ops:
  0.0 1.1 %copy-start.10 = (s32[8,256]{1,0:T(8,128)S(1)}, s32[8,256]{1,0:T(8,128)}, u32[]{:S(2)}) copy-start(s32[8,256]{1,0:T(8,128)} %constant.20.clone.pos_ref) | copy-start | bytes 24580
  0.0 1.1 %copy-start.1 = (bf16[2,64,1536]{2,1,0:T(8,128)(2,1)S(1)}, bf16[2,64,1536]{2,1,0:T(8,128)(2,1)}, u32[]{:S(2)}) copy-start(bf16[2,64,1536]{2,1,0:T(8,128)(2,1)} %qkv_ref.1) | copy-start | bytes 1179652
  1.0 0.9 %copy-start.2 = (bf16[320,144]{1,0:T(8,128)(2,1)S(1)}, bf16[320,144]{1,0:T(8,128)(2,1)}, u32[]{:S(2)}) copy-start(bf16[320,144]{1,0:T(8,128)(2,1)} %constant.14.clone.strip_ref) | copy-start | bytes 276484
  1.0 1.0 %copy-start.4 = (bf16[2,64,512]{2,1,0:T(8,128)(2,1)S(1)}, bf16[2,64,512]{2,1,0:T(8,128)(2,1)}, u32[]{:S(2)}) copy-start(bf16[2,64,512]{2,1,0:T(8,128)(2,1)} %outw_ref.1) | copy-start | bytes 393220
  2.0 1.1 %copy-start = (bf16[576,624]{1,0:T(8,128)(2,1)S(1)}, bf16[576,624]{1,0:T(8,128)(2,1)}, u32[]{:S(2)}) copy-start(bf16[576,624]{1,0:T(8,128)(2,1)} %constant.16.clone.key_ref) | copy-start | bytes 2156548
  3.1 0.9 %copy-start.3 = (s32[144,144]{1,0:T(8,128)S(1)}, s32[144,144]{1,0:T(8,128)}, u32[]{:S(2)}) copy-start(s32[144,144]{1,0:T(8,128)} %idx_ref.1) | copy-start | bytes 248836
  4.0 0.9 %copy-start.5 = (f32[2,759,16]{1,2,0:T(8,128)S(1)}, f32[2,759,16]{1,2,0:T(8,128)}, u32[]{:S(2)}) copy-start(f32[2,759,16]{1,2,0:T(8,128)} %param.18) | copy-start | bytes 291460
  4.9 0.9 %copy-start.6 = (bf16[192,256]{1,0:T(8,128)(2,1)S(1)}, bf16[192,256]{1,0:T(8,128)(2,1)}, u32[]{:S(2)}) copy-start(bf16[192,256]{1,0:T(8,128)(2,1)} %constant.19.clone.place_ref) | copy-start | bytes 294916
  5.8 0.9 %copy-start.7 = (bf16[192,144]{1,0:T(8,128)(2,1)S(1)}, bf16[192,144]{1,0:T(8,128)(2,1)}, u32[]{:S(2)}) copy-start(bf16[192,144]{1,0:T(8,128)(2,1)} %constant.17.clone.query_ref) | copy-start | bytes 165892
  6.7 0.9 %copy-start.8 = (bf16[160,160]{1,0:T(8,128)(2,1)S(1)}, bf16[160,160]{1,0:T(8,128)(2,1)}, u32[]{:S(2)}) copy-start(bf16[160,160]{1,0:T(8,128)(2,1)} %constant.15.clone.corner_ref) | copy-start | bytes 153604
  7.6 0.9 %copy-start.9 = (bf16[144,192]{1,0:T(8,128)(2,1)S(1)}, bf16[144,192]{1,0:T(8,128)(2,1)}, u32[]{:S(2)}) copy-start(bf16[144,192]{1,0:T(8,128)(2,1)} %constant.18.clone.back_ref) | copy-start | bytes 165892
  8.5 0.7 copy-start.11
  9.2 0.7 copy-start.12

commit v2 on v1

--- a/solution.py
+++ b/solution.py
@@ -118,12 +118,14 @@
 
 
 def kernel(
-    x_ref, gain_ref, qkv_ref, outw_ref, table_ref, idx_ref, region_ref,
+    x_hbm, gain_hbm, qkv_ref, outw_ref, table_hbm, idx_hbm, region_hbm,
+    strip_hbm, corner_hbm, key_hbm, query_hbm, back_hbm, place_hbm, pos_hbm,
+    out_ref,
+    x_ref, gain_ref, table_ref, idx_ref, region_ref,
     strip_ref, corner_ref, key_ref, query_ref, back_ref, place_ref, pos_ref,
-    out_ref,
     wq, wo, table, index, index_out, regions, tags, allowed,
     bias0, bias1, normed, qkv0, mixed0, middle, rows, strip_out, corner_out, xq, xk, q1, kv1, mixed1,
-    local_sem, send_sem, recv_sem,
+    load_sem, local_sem, send_sem, recv_sem,
     *, lat_count, lon_count,
 ):
     la, lo, fs = lax.axis_index("lat"), lax.axis_index("lon"), lax.axis_index("fsdp")
@@ -145,6 +147,16 @@
     for partner in partners:
         pl.semaphore_signal(barrier, inc=1, device_id=partner, device_id_type=MESH)
 
+    loads = []
+    for k, (source, target) in enumerate((
+        (table_hbm, table_ref), (idx_hbm, idx_ref), (x_hbm, x_ref), (gain_hbm, gain_ref), (region_hbm, region_ref),
+        (pos_hbm, pos_ref), (place_hbm, place_ref), (query_hbm, query_ref), (strip_hbm, strip_ref),
+        (corner_hbm, corner_ref), (key_hbm, key_ref), (back_hbm, back_ref),
+    )):
+        copy = pltpu.make_async_copy(source, target, load_sem.at[k])
+        copy.start()
+        loads.append(copy)
+
     counter = [0]
     sent = []
 
@@ -176,10 +188,6 @@
         copy.start()
         held.append(copy)
 
-    table[...] = jnp.zeros_like(table)
-    table[:, :, :BIAS_ROWS] = table_ref[...] * LOG2E
-    index[...] = jnp.zeros_like(index)
-    index[:, :WIN] = idx_ref[...]
     pl.semaphore_wait(barrier, len(partners))
 
     stages = {}
@@ -232,6 +240,13 @@
             stages[k][at].wait_recv()
 
     start_weights(0)
+
+    table[...] = jnp.zeros_like(table)
+    index[...] = jnp.zeros_like(index)
+    for copy in loads[:8]:
+        copy.wait()
+    table[:, :, :BIAS_ROWS] = table_ref[...] * LOG2E
+    index[:, :WIN] = idx_ref[...]
 
     region_rows = jnp.zeros((16, 128), F32)
     regions[...] = region_rows
@@ -250,20 +265,27 @@
 
     normed[...] = normalize(x_ref[...].astype(F32), gain_ref[0:1])
 
+    places = index[...]
+    index_lane = jnp.dot(place_ref[:, :WIN], (places & 127).astype(F32).astype(BF16), preferred_element_type=F32)
+    index_chunk = jnp.dot(place_ref[:, :WIN], (places >> 7).astype(F32).astype(BF16), preferred_element_type=F32)
+    index_out[...] = (index_chunk * 128.0 + index_lane).astype(jnp.int32)
+    def gathered(block, places):
+        lane = places & 127
+        chunk = places >> 7
+        masks = [chunk == c for c in range(1, 6)]
+        for h in range(HEADS):
+            total = None
+            for c in range(6):
+                piece = picked(jnp.broadcast_to(table[block, h : h + 1, c * 128 : c * 128 + 128], (8, 128)), lane)
+                total = piece if total is None else jnp.where(masks[c - 1], piece, total)
+            yield h, total
+
     def bias_rows0(first, count):
         @pl.loop(first, first + count)
         def _(r):
             span = pl.ds(pl.multiple_of(r * 8, 8), 8)
-            for side in range(2):
-                lanes = slice(side * 128, side * 128 + 128)
-                places = index[span, lanes]
-                lane = places & 127
-                chunk = places >> 7
-                for h in range(HEADS):
-                    total = None
-                    for c in range(6):
-                        piece = picked(jnp.broadcast_to(table[0, h : h + 1, c * 128 : c * 128 + 128], (8, 128)), lane)
-                        total = piece if total is None else jnp.where(chunk == c, piece, total)
+            for lanes in (slice(0, 128), slice(128, 256)):
+                for h, total in gathered(0, index[span, lanes]):
                     bias0[h, span, lanes] = total
 
     def bias_rows1(first, count):
@@ -272,27 +294,25 @@
             span = pl.ds(pl.multiple_of(r * 8, 8), 8)
             window = r // 6
             inner = pl.ds(pl.multiple_of((r % 6) * 8, 8), 8)
-            for side in range(2):
-                lanes = slice(side * 128, side * 128 + 128)
-                places = index_out[span, lanes]
-                lane = places & 127
-                chunk = places >> 7
+            for lanes in (slice(0, 128), slice(128, 256)):
                 keep = allowed[span, lanes] > 0.5
-                for h in range(HEADS):
-                    total = None
-                    for c in range(6):
-                        piece = picked(jnp.broadcast_to(table[1, h : h + 1, c * 128 : c * 128 + 128], (8, 128)), lane)
-                        total = piece if total is None else jnp.where(chunk == c, piece, total)
+                for h, total in gathered(1, index_out[span, lanes]):
                     bias1[window, h, inner, lanes] = jnp.where(keep, total, BLOCKED)
 
-    bias_rows0(0, 6)
+    bias_rows0(0, 9)
     pass_first(0)
     tag_south.wait_recv()
     tag_corner = send(tags.at[1], tags.at[0], east)
-    bias_rows0(6, 6)
+    bias_rows0(9, 9)
     pass_second(0)
     start_weights(1)
-    bias_rows0(12, 6)
+    tag_east.wait_recv()
+    tag_corner.wait_recv()
+    for w in range(4):
+        span = slice(w * QPAD, w * QPAD + QPAD)
+        query_tags = lax.dot_general(place_ref[span], tags[w].astype(BF16), (((1,), (1,)), ((), ())), preferred_element_type=F32)
+        allowed[span] = jnp.where(query_tags[:, 0:1] == tags[w, 0:1], 1.0, 0.0)
+    bias_rows1(0, 12)
     pass_across(0)
     finish_weights(0)
 
@@ -328,6 +348,8 @@
     pass_second(1)
     pass_across(1)
     finish_weights(1)
+    for copy in loads[8:]:
+        copy.wait()
     projected = jnp.dot(mixed0[...], wo[0], preferred_element_type=F32)
     mid = (x_ref[...].astype(F32) + projected).astype(BF16)
     middle[...] = mid
@@ -344,36 +366,24 @@
 
     pass_first(2)
     xq[...] = jnp.dot(query_ref[...], rows[0:WIN], preferred_element_type=F32).astype(BF16)
-    places = index[...]
-    index_lane = jnp.dot(place_ref[:, :WIN], (places & 127).astype(F32).astype(BF16), preferred_element_type=F32)
-    index_chunk = jnp.dot(place_ref[:, :WIN], (places >> 7).astype(F32).astype(BF16), preferred_element_type=F32)
-    index_out[...] = (index_chunk * 128.0 + index_lane).astype(jnp.int32)
-    tag_east.wait_recv()
-    tag_corner.wait_recv()
-    for w in range(4):
-        span = slice(w * QPAD, w * QPAD + QPAD)
-        query_tags = lax.dot_general(place_ref[span], tags[w].astype(BF16), (((1,), (1,)), ((), ())), preferred_element_type=F32)
-        allowed[span] = jnp.where(query_tags[:, 0:1] == tags[w, 0:1], 1.0, 0.0)
-    bias_rows1(0, 8)
+    bias_rows1(12, 6)
     pass_second(2)
     start_weights(3)
-    bias_rows1(8, 8)
+    bias_rows1(18, 6)
     pass_across(2)
+    finish_weights(2)
     pass_first(3)
+    @pl.loop(0, 2)
+    def _(t):
+        lanes = pl.ds(pl.multiple_of(t * 256, 256), 256)
+        q1[:, lanes] = jnp.dot(xq[...], wq[1, :, lanes], preferred_element_type=F32).astype(BF16)
+
     to_north.wait_recv()
     to_south.wait_recv()
     corner_out[...] = jnp.dot(corner_ref[...], rows[WIN : WIN + 2 * SPAD], preferred_element_type=F32).astype(BF16)
     corner_west = send(corner_out.at[pl.ds(0, SPAD)], slot(5), west)
     corner_east = send(corner_out.at[pl.ds(SPAD, SPAD)], slot(4), east)
-    bias_rows1(16, 8)
     pass_second(3)
-    finish_weights(2)
-
-    @pl.loop(0, 2)
-    def _(t):
-        lanes = pl.ds(pl.multiple_of(t * 256, 256), 256)
-        q1[:, lanes] = jnp.dot(xq[...], wq[1, :, lanes], preferred_element_type=F32).astype(BF16)
-
     pass_across(3)
     to_west.wait_recv()
     to_east.wait_recv()
@@ -426,14 +436,18 @@
 
 
 def local(lat_count, lon_count, latent, norm_gain, qkv_weight, out_weight, rel_bias, bias_index, region_ids):
+    operands = (
+        latent.reshape(WIN, D), norm_gain, qkv_weight, out_weight,
+        jnp.transpose(rel_bias, (0, 2, 1)), bias_index, jnp.transpose(region_ids, (1, 0, 2)),
+        *(jnp.asarray(s) for s in selections()),
+    )
     vmem = pl.BlockSpec(memory_space=pltpu.VMEM)
-    anywhere = pl.BlockSpec(memory_space=pl.ANY)
     out = pl.pallas_call(
         functools.partial(kernel, lat_count=lat_count, lon_count=lon_count),
         out_shape=jax.ShapeDtypeStruct((WIN, D), BF16),
-        in_specs=[vmem, vmem, anywhere, anywhere] + [vmem] * 10,
+        in_specs=[pl.BlockSpec(memory_space=pltpu.HBM)] * 14,
         out_specs=vmem,
-        scratch_shapes=[
+        scratch_shapes=[pltpu.VMEM(a.shape, a.dtype) for k, a in enumerate(operands) if k not in (2, 3)] + [
             pltpu.VMEM((2, D, 3 * D), BF16),
             pltpu.VMEM((2, D, D), BF16),
             pltpu.VMEM((2, HEADS, 768), F32),
@@ -456,19 +470,16 @@
             pltpu.VMEM((4 * QPAD, D), BF16),
             pltpu.VMEM((4 * WIN, 2 * D), BF16),
             pltpu.VMEM((4 * QPAD, D), BF16),
+            pltpu.SemaphoreType.DMA((12,)),
             pltpu.SemaphoreType.DMA((4,)),
             pltpu.SemaphoreType.DMA((COPIES,)),
             pltpu.SemaphoreType.DMA((COPIES,)),
         ],
         compiler_params=pltpu.CompilerParams(
-            collective_id=0, has_side_effects=True, vmem_limit_bytes=48 * 2**20
+            collective_id=0, has_side_effects=True, vmem_limit_bytes=60 * 2**20
         ),
         name="two_blocks",
-    )(
-        latent.reshape(WIN, D), norm_gain, qkv_weight, out_weight,
-        jnp.transpose(rel_bias, (0, 2, 1)), bias_index, jnp.transpose(region_ids, (1, 0, 2)),
-        *(jnp.asarray(s) for s in selections()),
-    )
+    )(*operands)
     return out.reshape(latent.shape)
 
 

time: 73.4 us -> 71.5 us (0.974)
  local copies, waits for them, and re-layouts: 10.7 us -> 3.39 us
  Pallas kernels: 62.2 us -> 67.9 us
    unnamed x27 -> x1, local copies, waits for them, and re-layouts: 9.77 us -> 0.93 us
    pallas_call x1, Pallas kernels: 62.2 us -> 67.9 us  [local(): pl.pallas_call(functools.partial(kernel, lat_count=lat_count, lon_count=l...]
    reshape x2, local copies, waits for them, and re-layouts: 0.85 us -> 1.76 us  [local(): return out.reshape(latent.shape)]
where the time goes in v2:
time: 71.5 us; the launch traced here: 71.3 us
  Pallas kernels  67.9 us (95%)
  local copies, waits for them, and re-layouts  3.39 us (5%)
    pallas_call x1, Pallas kernels, local(): pl.pallas_call(functools.partial(kernel, lat_count=lat_count, lon_count=l...  67.9 us
    reshape x2, local copies, waits for them, and re-layouts, local(): return out.reshape(latent.shape)  1.76 us

profile of v2, /device:TPU:1, one launch (start us, length us, event | category | flops | bytes accessed | tf_op | source)
XLA Modules:
  0.0 71.3 jit_solution(679596193338381741)
XLA Ops:
  0.0 0.9 %copy.17 = bf16[1,2,6,12,512]{4,3,2,1,0:T(8,128)(2,1)S(1)} copy(bf16[1,2,6,12,512]{4,1,3,2,0:T(2,128)(2,1)} %param.14) | data formatting | bytes 294912 | tf_op args[0]
  0.9 0.7 reshape.6.x_hbm
  1.6 67.9 %two_blocks.1 = bf16[144,512]{1,0:T(8,128)(2,1)} custom-call(bf16[144,512]{1,0:T(8,128)(2,1)} %reshape.6.x_hbm, f32[2,512]{1,0:T(2,128)} %gain_hbm.1, bf16[2,64,1536]{2,1,0:T(8,128)(2,1)} %qkv_ref.1, bf16[2,64,512]{2,1,0:T(8,128)(2,1)} %outw_ref.1, f32[2,16,759]{2,1,0:T(8,128)} %bitcast.2, s32[144,144]{1,0:T(8,128)} %idx_hbm.1, s32[6,2,12]{2,1,0:T(2,128)} %bitcast.3, ...), custom_call_target="tpu_custom_call" | custom-call | tf_op jit(solution)/shard_map/two_blocks/pallas_call | solution.py:445
  69.6 0.9 %reshape.7 = bf16[1,2,6,12,512]{4,3,2,1,0:T(8,128)(2,1)S(1)} reshape(bf16[144,512]{1,0:T(8,128)(2,1)} %two_blocks.1) | data formatting | bytes 294912 | tf_op jit(solution)/shard_map/reshape | solution.py:483
  70.5 0.8 %copy.18 = bf16[1,2,6,12,512]{4,1,3,2,0:T(2,128)(2,1)} copy(bf16[1,2,6,12,512]{4,3,2,1,0:T(8,128)(2,1)S(1)} %reshape.7) | data formatting | bytes 294912 | tf_op jit(solution)/shard_map/reshape | solution.py:483

commit v3 on v2

--- a/solution.py
+++ b/solution.py
@@ -18,9 +18,11 @@
 HH = WH // 2
 HW = WW // 2
 QUAD = WZ * HH * HW
-QPAD = 48
+QPAD = 40
 SPAD = 80
-ROWS = WIN + 6 * SPAD
+EARLY = 512
+ROWS = EARLY + 2 * SPAD
+SLOTS = tuple(WIN + k * SPAD for k in range(4)) + (EARLY, EARLY + SPAD)
 BIAS_ROWS = 759
 LOG2E = 1.4426950408889634
 SCALE = LOG2E * HEAD_DIM ** (-0.5)
@@ -64,7 +66,7 @@
     corners = one_hot_rows(corner(0) + corner(HW), 2 * SPAD, 2 * SPAD)
 
     def source(z, row, col):
-        n, s, w_, e, cw, ce = (WIN + k * SPAD for k in range(6))
+        n, s, w_, e, cw, ce = SLOTS
         if HH <= row < HH + WH:
             h = row - HH
             if col < HW:
@@ -123,7 +125,7 @@
     out_ref,
     x_ref, gain_ref, table_ref, idx_ref, region_ref,
     strip_ref, corner_ref, key_ref, query_ref, back_ref, place_ref, pos_ref,
-    wq, wo, table, index, index_out, regions, tags, allowed,
+    wide, wq, wo, table, index, index_out, regions, tags, allowed,
     bias0, bias1, normed, qkv0, mixed0, middle, rows, strip_out, corner_out, xq, xk, q1, kv1, mixed1,
     load_sem, local_sem, send_sem, recv_sem,
     *, lat_count, lon_count,
@@ -203,40 +205,31 @@
 
     def pass_first(k):
         full, _ = weights[k]
-        first, second = stages[k][0], stages[k][1]
-        first.wait_recv()
+        stages[k][0].wait_recv()
         low = part(full, from_right, half)
         relay_left = send(low, low, left)
-        share_low = send(low, low, sibling)
-        second.wait_recv()
+        stages[k][1].wait_recv()
         high = part(full, from_left + half, half)
         relay_right = send(high, high, right)
-        share_high = send(high, high, sibling)
-        stages[k] += [relay_left, relay_right, share_low, share_high]
+        stages[k] += [relay_left, relay_right]
 
     def pass_second(k):
         full, _ = weights[k]
-        stages[k][2].wait_recv()
-        high = part(full, from_right + half, half)
-        share_high = send(high, high, sibling)
-        stages[k][3].wait_recv()
-        low = part(full, from_left, half)
-        share_low = send(low, low, sibling)
-        stages[k] += [share_high, share_low]
+        for at, start in ((2, from_right), (3, from_left)):
+            stages[k][at].wait_recv()
+            whole = part(full, start, shard)
+            stages[k].append(send(whole, whole, sibling))
 
     def pass_across(k):
         full, _ = weights[k]
         stages[k][5].wait_recv()
-        low = part(full, across, half)
-        share_low = send(low, low, sibling)
         stages[k][6].wait_recv()
-        high = part(full, across + half, half)
-        share_high = send(high, high, sibling)
-        stages[k] += [share_low, share_high]
+        whole = part(full, across, shard)
+        stages[k].append(send(whole, whole, sibling))
 
     def finish_weights(k):
         held[k].wait()
-        for at in (4, 7, 8, 9, 10, 11, 12):
+        for at in (4, 7, 8, 9):
             stages[k][at].wait_recv()
 
     start_weights(0)
@@ -263,7 +256,9 @@
     tag_south = send(tags.at[3], tags.at[1], south)
     tag_east = send(tags.at[3], tags.at[2], east)
 
-    normed[...] = normalize(x_ref[...].astype(F32), gain_ref[0:1])
+    for i in range(WZ * WH):
+        wide[i * WW : i * WW + WW] = x_ref[i].astype(F32)
+    normed[...] = normalize(wide[...], gain_ref[0:1])
 
     places = index[...]
     index_lane = jnp.dot(place_ref[:, :WIN], (places & 127).astype(F32).astype(BF16), preferred_element_type=F32)
@@ -292,8 +287,8 @@
         @pl.loop(first, first + count)
         def _(r):
             span = pl.ds(pl.multiple_of(r * 8, 8), 8)
-            window = r // 6
-            inner = pl.ds(pl.multiple_of((r % 6) * 8, 8), 8)
+            window = r // 5
+            inner = pl.ds(pl.multiple_of((r % 5) * 8, 8), 8)
             for lanes in (slice(0, 128), slice(128, 256)):
                 keep = allowed[span, lanes] > 0.5
                 for h, total in gathered(1, index_out[span, lanes]):
@@ -301,18 +296,20 @@
 
     bias_rows0(0, 9)
     pass_first(0)
+    start_weights(1)
     tag_south.wait_recv()
     tag_corner = send(tags.at[1], tags.at[0], east)
     bias_rows0(9, 9)
     pass_second(0)
-    start_weights(1)
+    pass_first(1)
+    start_weights(2)
     tag_east.wait_recv()
     tag_corner.wait_recv()
     for w in range(4):
         span = slice(w * QPAD, w * QPAD + QPAD)
-        query_tags = lax.dot_general(place_ref[span], tags[w].astype(BF16), (((1,), (1,)), ((), ())), preferred_element_type=F32)
-        allowed[span] = jnp.where(query_tags[:, 0:1] == tags[w, 0:1], 1.0, 0.0)
-    bias_rows1(0, 12)
+        query_tags = lax.dot_general(place_ref[...], tags[w].astype(BF16), (((1,), (1,)), ((), ())), preferred_element_type=F32)
+        allowed[span] = jnp.where(query_tags[span, 0:1] == tags[w, 0:1], 1.0, 0.0)
+    bias_rows1(0, 6)
     pass_across(0)
     finish_weights(0)
 
@@ -321,14 +318,13 @@
         lanes = pl.ds(pl.multiple_of(t * 256, 256), 256)
         qkv0[:, lanes] = jnp.dot(normed[...], wq[0, :, lanes], preferred_element_type=F32).astype(BF16)
 
-    pass_first(1)
-    start_weights(2)
+    pass_second(1)
+    pass_across(1)
     lane_head = lax.broadcasted_iota(jnp.int32, (1, 128), 1) // HEAD_DIM
 
-    @pl.loop(0, 4)
-    def _(g):
+    def attend0(g):
         def cut(base):
-            return qkv0[:, pl.ds(pl.multiple_of(base + g * 128, 128), 128)]
+            return qkv0[:, base + g * 128 : base + g * 128 + 128]
 
         q, k, v = cut(0), cut(D), cut(2 * D)
         v_ones = jnp.concatenate([v, jnp.ones((WIN, 128), BF16)], axis=1)
@@ -343,57 +339,68 @@
             both = jnp.dot(weight, v_ones, preferred_element_type=F32)
             top = jnp.where(mine, both[:, :128], top)
             bottom = jnp.where(mine, both[:, 128:], bottom)
-        mixed0[:, pl.ds(pl.multiple_of(g * 128, 128), 128)] = (top / bottom).astype(BF16)
-
-    pass_second(1)
-    pass_across(1)
+        mixed0[:, g * 128 : g * 128 + 128] = (top / bottom).astype(BF16)
+
+    attend0(0)
+    attend0(1)
+    pass_first(2)
+    start_weights(3)
+    attend0(2)
+    attend0(3)
+
+    pass_second(2)
     finish_weights(1)
     for copy in loads[8:]:
         copy.wait()
     projected = jnp.dot(mixed0[...], wo[0], preferred_element_type=F32)
-    mid = (x_ref[...].astype(F32) + projected).astype(BF16)
+    mid = (wide[...] + projected).astype(BF16)
     middle[...] = mid
     rows[0:WIN] = normalize(mid.astype(F32), gain_ref[1:2])
     strip_out[...] = jnp.dot(strip_ref[...], rows[0:WIN], preferred_element_type=F32).astype(BF16)
 
     def slot(k):
-        return rows.at[pl.ds(WIN + k * SPAD, SPAD)]
+        return rows.at[pl.ds(SLOTS[k], SPAD)]
 
     to_north = send(strip_out.at[pl.ds(0, SPAD)], slot(1), north)
     to_south = send(strip_out.at[pl.ds(SPAD, SPAD)], slot(0), south)
     to_west = send(strip_out.at[pl.ds(2 * SPAD, SPAD)], slot(3), west)
     to_east = send(strip_out.at[pl.ds(3 * SPAD, SPAD)], slot(2), east)
 
-    pass_first(2)
+    pass_first(3)
     xq[...] = jnp.dot(query_ref[...], rows[0:WIN], preferred_element_type=F32).astype(BF16)
-    bias_rows1(12, 6)
-    pass_second(2)
-    start_weights(3)
-    bias_rows1(18, 6)
+    rows[SLOTS[3] + SPAD : EARLY] = jnp.zeros((EARLY - SLOTS[3] - SPAD, D), BF16)
     pass_across(2)
+    bias_rows1(6, 6)
     finish_weights(2)
-    pass_first(3)
+    pass_second(3)
+    pass_across(3)
+
     @pl.loop(0, 2)
     def _(t):
         lanes = pl.ds(pl.multiple_of(t * 256, 256), 256)
-        q1[:, lanes] = jnp.dot(xq[...], wq[1, :, lanes], preferred_element_type=F32).astype(BF16)
+        q1[:, lanes] = jnp.dot(xq[...], wq[1, :, lanes], preferred_element_type=F32)
 
     to_north.wait_recv()
     to_south.wait_recv()
     corner_out[...] = jnp.dot(corner_ref[...], rows[WIN : WIN + 2 * SPAD], preferred_element_type=F32).astype(BF16)
     corner_west = send(corner_out.at[pl.ds(0, SPAD)], slot(5), west)
     corner_east = send(corner_out.at[pl.ds(SPAD, SPAD)], slot(4), east)
-    pass_second(3)
-    pass_across(3)
+    bias_rows1(12, 8)
     to_west.wait_recv()
     to_east.wait_recv()
-    corner_west.wait_recv()
-    corner_east.wait_recv()
 
     @pl.loop(0, 4)
     def _(t):
         span = pl.ds(pl.multiple_of(t * WIN, 16), WIN)
-        xk[span] = jnp.dot(key_ref[span], rows[...], preferred_element_type=F32).astype(BF16)
+        xk[span] = jnp.dot(key_ref[span, :EARLY], rows[:EARLY], preferred_element_type=F32).astype(BF16)
+
+    corner_west.wait_recv()
+    corner_east.wait_recv()
+
+    @pl.loop(0, 4)
+    def _(t):
+        span = pl.ds(pl.multiple_of(t * WIN, 16), WIN)
+        xk[span] += jnp.dot(key_ref[span, EARLY:], rows[EARLY:], preferred_element_type=F32).astype(BF16)
 
     @pl.loop(0, 4)
     def _(t):
@@ -401,18 +408,18 @@
         source = pl.ds(pl.multiple_of(D + t * 256, 256), 256)
         kv1[:, lanes] = jnp.dot(xk[...], wq[1, :, source], preferred_element_type=F32).astype(BF16)
 
-    @pl.loop(0, 4)
-    def _(g):
+    def attend1(g):
+        lanes = slice(g * 128, g * 128 + 128)
         for w in range(4):
             span = slice(w * QPAD, w * QPAD + QPAD)
             keys = slice(w * WIN, w * WIN + WIN)
-            q = q1[span, pl.ds(pl.multiple_of(g * 128, 128), 128)]
-            k = kv1[keys, pl.ds(pl.multiple_of(g * 128, 128), 128)]
-            v = kv1[keys, pl.ds(pl.multiple_of(D + g * 128, 128), 128)]
+            q = q1[span, lanes]
+            k = kv1[keys, lanes]
+            v = kv1[keys, D + g * 128 : D + g * 128 + 128]
             v_ones = jnp.concatenate([v, jnp.ones((WIN, 128), BF16)], axis=1)
-            stacked = jnp.concatenate([jnp.where(lane_head == u, q, jnp.zeros_like(q)) for u in range(4)], axis=0)
+            stacked = jnp.concatenate([jnp.where(lane_head == u, q, 0.0) for u in range(4)], axis=0).astype(BF16)
             scores = lax.dot_general(stacked, k, (((1,), (1,)), ((), ())), preferred_element_type=F32)
-            bias = bias1[w, pl.ds(g * 4, 4), :, :WIN].reshape(4 * QPAD, WIN)
+            bias = bias1[w, g * 4 : g * 4 + 4, :, :WIN].reshape(4 * QPAD, WIN)
             scores = scores * SCALE + bias
             peak = jnp.max(scores, axis=1, keepdims=True)
             weight = jnp.exp2(scores - peak).astype(BF16)
@@ -422,32 +429,38 @@
                 mine = lane_head == u
                 top = jnp.where(mine, both[u * QPAD : u * QPAD + QPAD, :128], top)
                 bottom = jnp.where(mine, both[u * QPAD : u * QPAD + QPAD, 128:], bottom)
-            mixed1[span, pl.ds(pl.multiple_of(g * 128, 128), 128)] = (top / bottom).astype(BF16)
+            mixed1[span, lanes] = top / bottom
+
+    for g in range(4):
+        attend1(g)
 
     finish_weights(3)
-    natural = jnp.dot(back_ref[...], mixed1[...], preferred_element_type=F32).astype(BF16)
+    natural = jnp.dot(back_ref[...], mixed1[...].astype(BF16), preferred_element_type=F32).astype(BF16)
     projected = jnp.dot(natural, wo[1], preferred_element_type=F32)
-    out_ref[...] = (middle[...].astype(F32) + projected).astype(BF16)
+    wide[...] = middle[...].astype(F32) + projected
+    for i in range(WZ * WH):
+        out_ref[i] = wide[i * WW : i * WW + WW].astype(BF16)
     for copy in sent:
         copy.wait_send()
 
 
-COPIES = 4 * 13 + 3 + 6
+COPIES = 4 * 10 + 3 + 6
 
 
 def local(lat_count, lon_count, latent, norm_gain, qkv_weight, out_weight, rel_bias, bias_index, region_ids):
     operands = (
-        latent.reshape(WIN, D), norm_gain, qkv_weight, out_weight,
+        latent.reshape(WZ * WH, WW, D), norm_gain, qkv_weight, out_weight,
         jnp.transpose(rel_bias, (0, 2, 1)), bias_index, jnp.transpose(region_ids, (1, 0, 2)),
         *(jnp.asarray(s) for s in selections()),
     )
     vmem = pl.BlockSpec(memory_space=pltpu.VMEM)
     out = pl.pallas_call(
         functools.partial(kernel, lat_count=lat_count, lon_count=lon_count),
-        out_shape=jax.ShapeDtypeStruct((WIN, D), BF16),
+        out_shape=jax.ShapeDtypeStruct((WZ * WH, WW, D), BF16),
         in_specs=[pl.BlockSpec(memory_space=pltpu.HBM)] * 14,
         out_specs=vmem,
         scratch_shapes=[pltpu.VMEM(a.shape, a.dtype) for k, a in enumerate(operands) if k not in (2, 3)] + [
+            pltpu.VMEM((WIN, D), F32),
             pltpu.VMEM((2, D, 3 * D), BF16),
             pltpu.VMEM((2, D, D), BF16),
             pltpu.VMEM((2, HEADS, 768), F32),
@@ -467,9 +480,9 @@
             pltpu.VMEM((2 * SPAD, D), BF16),
             pltpu.VMEM((4 * QPAD, D), BF16),
             pltpu.VMEM((4 * WIN, D), BF16),
-            pltpu.VMEM((4 * QPAD, D), BF16),
+            pltpu.VMEM((4 * QPAD, D), F32),
             pltpu.VMEM((4 * WIN, 2 * D), BF16),
-            pltpu.VMEM((4 * QPAD, D), BF16),
+            pltpu.VMEM((4 * QPAD, D), F32),
             pltpu.SemaphoreType.DMA((12,)),
             pltpu.SemaphoreType.DMA((4,)),
             pltpu.SemaphoreType.DMA((COPIES,)),

time: 71.5 us -> 64.4 us (0.901)
  Pallas kernels: 67.9 us -> 60.8 us
    pallas_call x1, Pallas kernels: 67.9 us -> 60.8 us  [local(): pl.pallas_call(functools.partial(kernel, lat_count=lat_count, lon_count=l...]
    reshape x2 -> x1, local copies, waits for them, and re-layouts: 1.76 us -> 1.74 us  [local(): return out.reshape(latent.shape)]
where the time goes in v3:
time: 64.4 us; the launch traced here: 64.2 us
  Pallas kernels  60.8 us (94%)
  local copies, waits for them, and re-layouts  3.35 us (5%)
    pallas_call x1, Pallas kernels, local(): pl.pallas_call(functools.partial(kernel, lat_count=lat_count, lon_count=l...  60.8 us
    reshape x1, local copies, waits for them, and re-layouts, local(): return out.reshape(latent.shape)  1.74 us
    unnamed x1, local copies, waits for them, and re-layouts  1.61 us

profile of v3, /device:TPU:1, one launch (start us, length us, event | category | flops | bytes accessed | tf_op | source)
XLA Modules:
  0.0 64.2 jit_solution(1427486323633736807)
XLA Ops:
  0.0 1.6 %copy.15 = bf16[1,2,6,12,512]{4,3,2,1,0:T(8,128)(2,1)} copy(bf16[1,2,6,12,512]{4,1,3,2,0:T(2,128)(2,1)} %param.14) | data formatting | bytes 294912 | tf_op args[0]
  1.6 60.8 %two_blocks.1 = bf16[12,12,512]{2,1,0:T(8,128)(2,1)} custom-call(bf16[12,12,512]{2,1,0:T(8,128)(2,1)} %bitcast.5, f32[2,512]{1,0:T(2,128)} %gain_hbm.1, bf16[2,64,1536]{2,1,0:T(8,128)(2,1)} %qkv_ref.1, bf16[2,64,512]{2,1,0:T(8,128)(2,1)} %outw_ref.1, f32[2,16,759]{2,1,0:T(8,128)} %bitcast.6, s32[144,144]{1,0:T(8,128)} %idx_hbm.1, s32[6,2,12]{2,1,0:T(2,128)} %bitcast.7, ...), custom_call_target="tpu_custom_call" | custom-call | tf_op jit(solution)/shard_map/two_blocks/pallas_call | solution.py:457
  62.4 1.7 %copy.16 = bf16[1,2,6,12,512]{4,1,3,2,0:T(2,128)(2,1)} copy(bf16[1,2,6,12,512]{4,3,2,1,0:T(8,128)(2,1)} %bitcast.4) | data formatting | bytes 294912 | tf_op jit(solution)/shard_map/reshape | solution.py:496

commit v4 on v3

--- a/solution.py
+++ b/solution.py
@@ -20,6 +20,7 @@
 QUAD = WZ * HH * HW
 QPAD = 40
 SPAD = 80
+CUT = 48
 EARLY = 512
 ROWS = EARLY + 2 * SPAD
 SLOTS = tuple(WIN + k * SPAD for k in range(4)) + (EARLY, EARLY + SPAD)
@@ -127,16 +128,16 @@
     strip_ref, corner_ref, key_ref, query_ref, back_ref, place_ref, pos_ref,
     wide, wq, wo, table, index, index_out, regions, tags, allowed,
     bias0, bias1, normed, qkv0, mixed0, middle, rows, strip_out, corner_out, xq, xk, q1, kv1, mixed1,
-    load_sem, local_sem, send_sem, recv_sem,
+    load_sem, local_sem, send_sem, recv_sem, relay,
     *, lat_count, lon_count,
 ):
     la, lo, fs = lax.axis_index("lat"), lax.axis_index("lon"), lax.axis_index("fsdp")
     y_count = lat_count // 2
     y, core, x = la % y_count, fs % 2, (la // y_count) * 4 + fs // 2
 
-    def along_x(step):
+    def along_x(step, row=y):
         there = (x + step) % 8
-        return ((there // 4) * y_count + y, lo, (there % 4) * 2 + core)
+        return ((there // 4) * y_count + row, lo, (there % 4) * 2 + core)
 
     right, left = along_x(1), along_x(7)
     sibling = (la, lo, fs + 1 - 2 * core)
@@ -144,10 +145,20 @@
     south = ((la + 1) % lat_count, lo, fs)
     west = (la, (lo + lon_count - 1) % lon_count, fs)
     east = (la, (lo + 1) % lon_count, fs)
+    first_row, last_row = y == 0, y == y_count - 1
+    edge = jnp.logical_or(first_row, last_row)
+    ahead, behind = along_x(2), along_x(6)
+    far_ahead, far_behind = along_x(2, y_count - 1 - y), along_x(6, y_count - 1 - y)
     partners = (right, left, sibling, north, south, west, east)
+    edge_partners = (ahead, behind, far_ahead, far_behind)
     barrier = pltpu.get_barrier_semaphore()
     for partner in partners:
         pl.semaphore_signal(barrier, inc=1, device_id=partner, device_id_type=MESH)
+
+    @pl.when(edge)
+    def _():
+        for partner in edge_partners:
+            pl.semaphore_signal(barrier, inc=1, device_id=partner, device_id_type=MESH)
 
     loads = []
     for k, (source, target) in enumerate((
@@ -190,7 +201,13 @@
         copy.start()
         held.append(copy)
 
-    pl.semaphore_wait(barrier, len(partners))
+    @pl.when(edge)
+    def _():
+        pl.semaphore_wait(barrier, len(partners) + len(edge_partners))
+
+    @pl.when(jnp.logical_not(edge))
+    def _():
+        pl.semaphore_wait(barrier, len(partners))
 
     stages = {}
 
@@ -256,8 +273,9 @@
     tag_south = send(tags.at[3], tags.at[1], south)
     tag_east = send(tags.at[3], tags.at[2], east)
 
-    for i in range(WZ * WH):
-        wide[i * WW : i * WW + WW] = x_ref[i].astype(F32)
+    both_levels = x_ref[...].astype(F32)
+    for z in range(WZ):
+        wide[z * WH * WW : z * WH * WW + WH * WW] = both_levels[:, z, :]
     normed[...] = normalize(wide[...], gain_ref[0:1])
 
     places = index[...]
@@ -361,8 +379,48 @@
     def slot(k):
         return rows.at[pl.ds(SLOTS[k], SPAD)]
 
-    to_north = send(strip_out.at[pl.ds(0, SPAD)], slot(1), north)
-    to_south = send(strip_out.at[pl.ds(SPAD, SPAD)], slot(0), south)
+    def piece_copy(source, target, at, device):
+        return pltpu.make_async_remote_copy(
+            src_ref=source, dst_ref=target, send_sem=send_sem.at[at], recv_sem=recv_sem.at[at],
+            device_id=device, device_id_type=MESH,
+        )
+
+    pieces = (pl.ds(0, CUT), pl.ds(CUT, SPAD - CUT))
+    direct = []
+    routes = []
+    for base, target, neighbour, at_edge in ((0, 1, north, first_row), (SPAD, 0, south, last_row)):
+        own = []
+        first = []
+        second = []
+        for n, p in enumerate(pieces):
+            at = COPIES + 2 + len(direct)
+            source = strip_out.at[pl.ds(base + p.start, p.size)]
+            goal = rows.at[pl.ds(SLOTS[target] + p.start, p.size)]
+            own.append(piece_copy(source, goal, at, neighbour))
+            first.append(piece_copy(source, relay.at[p], COPIES + n, (ahead, behind)[n]))
+            second.append(piece_copy(relay.at[p], goal, at, (far_ahead, far_behind)[n]))
+            direct.append(own[-1])
+        routes.append((at_edge, own, first, second))
+
+    for at_edge, own, first, second in routes:
+        @pl.when(at_edge)
+        def _(first=first):
+            for copy in first:
+                copy.start()
+
+        @pl.when(jnp.logical_not(at_edge))
+        def _(own=own):
+            for copy in own:
+                copy.start()
+
+    def pass_halo():
+        for at_edge, own, first, second in routes:
+            @pl.when(at_edge)
+            def _(first=first, second=second):
+                for arrived, onward in zip(first, second):
+                    arrived.wait_recv()
+                    onward.start()
+
     to_west = send(strip_out.at[pl.ds(2 * SPAD, SPAD)], slot(3), west)
     to_east = send(strip_out.at[pl.ds(3 * SPAD, SPAD)], slot(2), east)
 
@@ -370,22 +428,24 @@
     xq[...] = jnp.dot(query_ref[...], rows[0:WIN], preferred_element_type=F32).astype(BF16)
     rows[SLOTS[3] + SPAD : EARLY] = jnp.zeros((EARLY - SLOTS[3] - SPAD, D), BF16)
     pass_across(2)
-    bias_rows1(6, 6)
+    bias_rows1(6, 7)
+    pass_halo()
     finish_weights(2)
     pass_second(3)
     pass_across(3)
+    bias_rows1(13, 5)
 
     @pl.loop(0, 2)
     def _(t):
         lanes = pl.ds(pl.multiple_of(t * 256, 256), 256)
         q1[:, lanes] = jnp.dot(xq[...], wq[1, :, lanes], preferred_element_type=F32)
 
-    to_north.wait_recv()
-    to_south.wait_recv()
+    for copy in direct:
+        copy.wait_recv()
     corner_out[...] = jnp.dot(corner_ref[...], rows[WIN : WIN + 2 * SPAD], preferred_element_type=F32).astype(BF16)
     corner_west = send(corner_out.at[pl.ds(0, SPAD)], slot(5), west)
     corner_east = send(corner_out.at[pl.ds(SPAD, SPAD)], slot(4), east)
-    bias_rows1(12, 8)
+    bias_rows1(18, 2)
     to_west.wait_recv()
     to_east.wait_recv()
 
@@ -437,26 +497,30 @@
     finish_weights(3)
     natural = jnp.dot(back_ref[...], mixed1[...].astype(BF16), preferred_element_type=F32).astype(BF16)
     projected = jnp.dot(natural, wo[1], preferred_element_type=F32)
-    wide[...] = middle[...].astype(F32) + projected
-    for i in range(WZ * WH):
-        out_ref[i] = wide[i * WW : i * WW + WW].astype(BF16)
-    for copy in sent:
+    total = middle[...].astype(F32) + projected
+    out_ref[...] = jnp.stack([total[: WH * WW], total[WH * WW :]], axis=1).astype(BF16)
+    for copy in sent + direct:
         copy.wait_send()
-
-
-COPIES = 4 * 10 + 3 + 6
+    for at_edge, own, first, second in routes:
+        @pl.when(at_edge)
+        def _(first=first):
+            for copy in first:
+                copy.wait_send()
+
+
+COPIES = 4 * 10 + 3 + 4
 
 
 def local(lat_count, lon_count, latent, norm_gain, qkv_weight, out_weight, rel_bias, bias_index, region_ids):
     operands = (
-        latent.reshape(WZ * WH, WW, D), norm_gain, qkv_weight, out_weight,
+        jnp.transpose(latent, (0, 2, 3, 1, 4)).reshape(WH * WW, WZ, D), norm_gain, qkv_weight, out_weight,
         jnp.transpose(rel_bias, (0, 2, 1)), bias_index, jnp.transpose(region_ids, (1, 0, 2)),
         *(jnp.asarray(s) for s in selections()),
     )
     vmem = pl.BlockSpec(memory_space=pltpu.VMEM)
     out = pl.pallas_call(
         functools.partial(kernel, lat_count=lat_count, lon_count=lon_count),
-        out_shape=jax.ShapeDtypeStruct((WZ * WH, WW, D), BF16),
+        out_shape=jax.ShapeDtypeStruct((WH * WW, WZ, D), BF16),
         in_specs=[pl.BlockSpec(memory_space=pltpu.HBM)] * 14,
         out_specs=vmem,
         scratch_shapes=[pltpu.VMEM(a.shape, a.dtype) for k, a in enumerate(operands) if k not in (2, 3)] + [
@@ -485,15 +549,16 @@
             pltpu.VMEM((4 * QPAD, D), F32),
             pltpu.SemaphoreType.DMA((12,)),
             pltpu.SemaphoreType.DMA((4,)),
-            pltpu.SemaphoreType.DMA((COPIES,)),
-            pltpu.SemaphoreType.DMA((COPIES,)),
+            pltpu.SemaphoreType.DMA((COPIES + 6,)),
+            pltpu.SemaphoreType.DMA((COPIES + 6,)),
+            pltpu.VMEM((SPAD, D), BF16),
         ],
         compiler_params=pltpu.CompilerParams(
             collective_id=0, has_side_effects=True, vmem_limit_bytes=60 * 2**20
         ),
         name="two_blocks",
     )(*operands)
-    return out.reshape(latent.shape)
+    return jnp.transpose(out.reshape(1, WH, WW, WZ, D), (0, 3, 1, 2, 4))
 
 
 def solution(mesh):

time: 64.4 us -> 63.6 us (0.988)
  local copies, waits for them, and re-layouts: 3.35 us -> 1.67 us
  Pallas kernels: 60.8 us -> 61.7 us
    reshape x1 -> x0, local copies, waits for them, and re-layouts: 1.74 us -> none  [local(): return out.reshape(latent.shape)]
    pallas_call x1, Pallas kernels: 60.8 us -> 61.7 us  [local(): pl.pallas_call(functools.partial(kernel, lat_count=lat_count, lon_count=l...]
where the time goes in v4:
time: 63.6 us; the launch traced here: 63.4 us
  Pallas kernels  61.7 us (97%)
  local copies, waits for them, and re-layouts  1.67 us (3%)
    pallas_call x1, Pallas kernels, local(): pl.pallas_call(functools.partial(kernel, lat_count=lat_count, lon_count=l...  61.7 us
    unnamed x1, local copies, waits for them, and re-layouts  1.67 us

profile of v4, /device:TPU:1, one launch (start us, length us, event | category | flops | bytes accessed | tf_op | source)
XLA Modules:
  0.0 63.4 jit_solution(8727505629079806042)
XLA Ops:
  0.0 61.7 %two_blocks.1 = bf16[72,2,512]{2,1,0:T(2,128)(2,1)} custom-call(bf16[72,2,512]{2,1,0:T(2,128)(2,1)} %bitcast.9, f32[2,512]{1,0:T(2,128)} %gain_hbm.1, bf16[2,64,1536]{2,1,0:T(8,128)(2,1)} %qkv_ref.1, bf16[2,64,512]{2,1,0:T(8,128)(2,1)} %outw_ref.1, f32[2,16,759]{2,1,0:T(8,128)} %bitcast.10, s32[144,144]{1,0:T(8,128)} %idx_hbm.1, s32[6,2,12]{2,1,0:T(2,128)} %bitcast.11, ...), custom_call_target="tpu_custom_call" | custom-call | tf_op jit(solution)/shard_map/two_blocks/pallas_call | solution.py:521
  61.7 1.7 %copy.16 = bf16[1,2,6,12,512]{4,1,3,2,0:T(2,128)(2,1)} copy(bf16[1,2,6,12,512]{4,1,3,2,0:T(2,128)(2,1)} %bitcast.8) | data formatting | bytes 294912

commit v5 on v3

--- a/solution.py
+++ b/solution.py
@@ -20,9 +20,10 @@
 QUAD = WZ * HH * HW
 QPAD = 40
 SPAD = 80
+CPAD = 48
 EARLY = 512
-ROWS = EARLY + 2 * SPAD
-SLOTS = tuple(WIN + k * SPAD for k in range(4)) + (EARLY, EARLY + SPAD)
+ROWS = EARLY + 4 * CPAD
+SLOTS = tuple(WIN + k * SPAD for k in range(4)) + (EARLY, EARLY + 2 * CPAD)
 BIAS_ROWS = 759
 LOG2E = 1.4426950408889634
 SCALE = LOG2E * HEAD_DIM ** (-0.5)
@@ -55,15 +56,10 @@
     strips = one_hot_rows(north + south + west + east, 4 * SPAD, WIN)
 
     def corner(first):
-        rows = []
-        for side in range(2):
-            for z in range(WZ):
-                for h in range(HH):
-                    for w in range(HW):
-                        rows.append(side * SPAD + (z * HH + h) * WW + first + w)
-        return rows + pad
-
-    corners = one_hot_rows(corner(0) + corner(HW), 2 * SPAD, 2 * SPAD)
+        rows = [(z * HH + h) * WW + first + w for z in range(WZ) for h in range(HH) for w in range(HW)]
+        return rows + [-1] * (CPAD - QUAD)
+
+    corners = one_hot_rows(corner(0) + corner(HW), 2 * CPAD, SPAD)
 
     def source(z, row, col):
         n, s, w_, e, cw, ce = SLOTS
@@ -77,10 +73,10 @@
         side = 0 if row < HH else 1
         h = row if row < HH else row - HH - WH
         if col < HW:
-            return cw + side * QUAD + (z * HH + h) * HW + col
+            return cw + side * CPAD + (z * HH + h) * HW + col
         if col < HW + WW:
             return (n, s)[side] + (z * HH + h) * WW + col - HW
-        return ce + side * QUAD + (z * HH + h) * HW + col - HW - WW
+        return ce + side * CPAD + (z * HH + h) * HW + col - HW - WW
 
     keys = []
     query_token = []
@@ -125,7 +121,7 @@
     out_ref,
     x_ref, gain_ref, table_ref, idx_ref, region_ref,
     strip_ref, corner_ref, key_ref, query_ref, back_ref, place_ref, pos_ref,
-    wide, wq, wo, table, index, index_out, regions, tags, allowed,
+    wide, partial, wq, wo, table, index, index_out, regions, tags, allowed,
     bias0, bias1, normed, qkv0, mixed0, middle, rows, strip_out, corner_out, xq, xk, q1, kv1, mixed1,
     load_sem, local_sem, send_sem, recv_sem,
     *, lat_count, lon_count,
@@ -256,8 +252,9 @@
     tag_south = send(tags.at[3], tags.at[1], south)
     tag_east = send(tags.at[3], tags.at[2], east)
 
-    for i in range(WZ * WH):
-        wide[i * WW : i * WW + WW] = x_ref[i].astype(F32)
+    both_levels = x_ref[...].astype(F32)
+    for z in range(WZ):
+        wide[z * WH * WW : z * WH * WW + WH * WW] = both_levels[:, z, :]
     normed[...] = normalize(wide[...], gain_ref[0:1])
 
     places = index[...]
@@ -310,13 +307,25 @@
         query_tags = lax.dot_general(place_ref[...], tags[w].astype(BF16), (((1,), (1,)), ((), ())), preferred_element_type=F32)
         allowed[span] = jnp.where(query_tags[span, 0:1] == tags[w, 0:1], 1.0, 0.0)
     bias_rows1(0, 6)
+    held[0].wait()
+    for at in (4, 7, 8):
+        stages[0][at].wait_recv()
+    chip = 2 * shard
+    own_chip = fs // 2
+
+    def chip_product(step, lanes):
+        start = pl.multiple_of(((own_chip + step) % 4) * chip, chip)
+        return jnp.dot(normed[:, pl.ds(start, chip)], wq[0, pl.ds(start, chip), lanes], preferred_element_type=F32)
+
+    for t in range(6):
+        lanes = slice(t * 256, t * 256 + 256)
+        partial[:, lanes] = chip_product(0, lanes) + chip_product(1, lanes) + chip_product(3, lanes)
     pass_across(0)
-    finish_weights(0)
-
-    @pl.loop(0, 6)
-    def _(t):
-        lanes = pl.ds(pl.multiple_of(t * 256, 256), 256)
-        qkv0[:, lanes] = jnp.dot(normed[...], wq[0, :, lanes], preferred_element_type=F32).astype(BF16)
+    stages[0][9].wait_recv()
+
+    for t in range(6):
+        lanes = slice(t * 256, t * 256 + 256)
+        qkv0[:, lanes] = (partial[:, lanes] + chip_product(2, lanes)).astype(BF16)
 
     pass_second(1)
     pass_across(1)
@@ -344,7 +353,6 @@
     attend0(0)
     attend0(1)
     pass_first(2)
-    start_weights(3)
     attend0(2)
     attend0(3)
 
@@ -366,26 +374,34 @@
     to_west = send(strip_out.at[pl.ds(2 * SPAD, SPAD)], slot(3), west)
     to_east = send(strip_out.at[pl.ds(3 * SPAD, SPAD)], slot(2), east)
 
-    pass_first(3)
+    start_weights(3)
     xq[...] = jnp.dot(query_ref[...], rows[0:WIN], preferred_element_type=F32).astype(BF16)
     rows[SLOTS[3] + SPAD : EARLY] = jnp.zeros((EARLY - SLOTS[3] - SPAD, D), BF16)
     pass_across(2)
-    bias_rows1(6, 6)
+    bias_rows1(6, 7)
     finish_weights(2)
-    pass_second(3)
-    pass_across(3)
+    pass_first(3)
+    bias_rows1(13, 5)
 
     @pl.loop(0, 2)
     def _(t):
         lanes = pl.ds(pl.multiple_of(t * 256, 256), 256)
         q1[:, lanes] = jnp.dot(xq[...], wq[1, :, lanes], preferred_element_type=F32)
 
-    to_north.wait_recv()
-    to_south.wait_recv()
-    corner_out[...] = jnp.dot(corner_ref[...], rows[WIN : WIN + 2 * SPAD], preferred_element_type=F32).astype(BF16)
-    corner_west = send(corner_out.at[pl.ds(0, SPAD)], slot(5), west)
-    corner_east = send(corner_out.at[pl.ds(SPAD, SPAD)], slot(4), east)
-    bias_rows1(12, 8)
+    corner_copies = []
+    for side, arrived in ((0, to_south), (1, to_north)):
+        arrived.wait_recv()
+        strip = rows[SLOTS[side] : SLOTS[side] + SPAD]
+        pieces = jnp.dot(corner_ref[...], strip, preferred_element_type=F32).astype(BF16)
+        first = side * 2 * CPAD
+        corner_out[first : first + 2 * CPAD] = pieces
+        for n, (start, device) in enumerate(((SLOTS[5], west), (SLOTS[4], east))):
+            corner_copies.append(send(
+                corner_out.at[pl.ds(first + n * CPAD, CPAD)], rows.at[pl.ds(start + side * CPAD, CPAD)], device
+            ))
+    pass_second(3)
+    pass_across(3)
+    bias_rows1(18, 2)
     to_west.wait_recv()
     to_east.wait_recv()
 
@@ -394,8 +410,8 @@
         span = pl.ds(pl.multiple_of(t * WIN, 16), WIN)
         xk[span] = jnp.dot(key_ref[span, :EARLY], rows[:EARLY], preferred_element_type=F32).astype(BF16)
 
-    corner_west.wait_recv()
-    corner_east.wait_recv()
+    for copy in corner_copies:
+        copy.wait_recv()
 
     @pl.loop(0, 4)
     def _(t):
@@ -437,30 +453,30 @@
     finish_weights(3)
     natural = jnp.dot(back_ref[...], mixed1[...].astype(BF16), preferred_element_type=F32).astype(BF16)
     projected = jnp.dot(natural, wo[1], preferred_element_type=F32)
-    wide[...] = middle[...].astype(F32) + projected
-    for i in range(WZ * WH):
-        out_ref[i] = wide[i * WW : i * WW + WW].astype(BF16)
+    total = middle[...].astype(F32) + projected
+    out_ref[...] = jnp.stack([total[: WH * WW], total[WH * WW :]], axis=1).astype(BF16)
     for copy in sent:
         copy.wait_send()
 
 
-COPIES = 4 * 10 + 3 + 6
+COPIES = 4 * 10 + 3 + 8
 
 
 def local(lat_count, lon_count, latent, norm_gain, qkv_weight, out_weight, rel_bias, bias_index, region_ids):
     operands = (
-        latent.reshape(WZ * WH, WW, D), norm_gain, qkv_weight, out_weight,
+        jnp.transpose(latent, (0, 2, 3, 1, 4)).reshape(WH * WW, WZ, D), norm_gain, qkv_weight, out_weight,
         jnp.transpose(rel_bias, (0, 2, 1)), bias_index, jnp.transpose(region_ids, (1, 0, 2)),
         *(jnp.asarray(s) for s in selections()),
     )
     vmem = pl.BlockSpec(memory_space=pltpu.VMEM)
     out = pl.pallas_call(
         functools.partial(kernel, lat_count=lat_count, lon_count=lon_count),
-        out_shape=jax.ShapeDtypeStruct((WZ * WH, WW, D), BF16),
+        out_shape=jax.ShapeDtypeStruct((WH * WW, WZ, D), BF16),
         in_specs=[pl.BlockSpec(memory_space=pltpu.HBM)] * 14,
         out_specs=vmem,
         scratch_shapes=[pltpu.VMEM(a.shape, a.dtype) for k, a in enumerate(operands) if k not in (2, 3)] + [
             pltpu.VMEM((WIN, D), F32),
+            pltpu.VMEM((WIN, 3 * D), F32),
             pltpu.VMEM((2, D, 3 * D), BF16),
             pltpu.VMEM((2, D, D), BF16),
             pltpu.VMEM((2, HEADS, 768), F32),
@@ -477,7 +493,7 @@
             pltpu.VMEM((WIN, D), BF16),
             pltpu.VMEM((ROWS, D), BF16),
             pltpu.VMEM((4 * SPAD, D), BF16),
-            pltpu.VMEM((2 * SPAD, D), BF16),
+            pltpu.VMEM((4 * CPAD, D), BF16),
             pltpu.VMEM((4 * QPAD, D), BF16),
             pltpu.VMEM((4 * WIN, D), BF16),
             pltpu.VMEM((4 * QPAD, D), F32),
@@ -493,7 +509,7 @@
         ),
         name="two_blocks",
     )(*operands)
-    return out.reshape(latent.shape)
+    return jnp.transpose(out.reshape(1, WH, WW, WZ, D), (0, 3, 1, 2, 4))
 
 
 def solution(mesh):

time: 64.4 us -> 61.5 us (0.955)
  local copies, waits for them, and re-layouts: 3.35 us -> 1.67 us
  Pallas kernels: 60.8 us -> 59.6 us
    reshape x1 -> x0, local copies, waits for them, and re-layouts: 1.74 us -> none  [local(): return out.reshape(latent.shape)]
    pallas_call x1, Pallas kernels: 60.8 us -> 59.6 us  [local(): pl.pallas_call(functools.partial(kernel, lat_count=lat_count, lon_count=l...]
where the time goes in v5:
time: 61.5 us; the launch traced here: 61.3 us
  Pallas kernels  59.6 us (97%)
  local copies, waits for them, and re-layouts  1.67 us (3%)
    pallas_call x1, Pallas kernels, local(): pl.pallas_call(functools.partial(kernel, lat_count=lat_count, lon_count=l...  59.6 us
    unnamed x1, local copies, waits for them, and re-layouts  1.67 us

profile of v5, /device:TPU:1, one launch (start us, length us, event | category | flops | bytes accessed | tf_op | source)
XLA Modules:
  0.0 61.3 jit_solution(5335509612180301806)
XLA Ops:
  0.0 59.6 %two_blocks.1 = bf16[72,2,512]{2,1,0:T(2,128)(2,1)} custom-call(bf16[72,2,512]{2,1,0:T(2,128)(2,1)} %bitcast.9, f32[2,512]{1,0:T(2,128)} %gain_hbm.1, bf16[2,64,1536]{2,1,0:T(8,128)(2,1)} %qkv_ref.1, bf16[2,64,512]{2,1,0:T(8,128)(2,1)} %outw_ref.1, f32[2,16,759]{2,1,0:T(8,128)} %bitcast.10, s32[144,144]{1,0:T(8,128)} %idx_hbm.1, s32[6,2,12]{2,1,0:T(2,128)} %bitcast.11, ...), custom_call_target="tpu_custom_call" | custom-call | tf_op jit(solution)/shard_map/two_blocks/pallas_call | solution.py:472
  59.7 1.7 %copy.16 = bf16[1,2,6,12,512]{4,1,3,2,0:T(2,128)(2,1)} copy(bf16[1,2,6,12,512]{4,1,3,2,0:T(2,128)(2,1)} %bitcast.8) | data formatting | bytes 294912

commit v6 on v5

--- a/solution.py
+++ b/solution.py
@@ -22,8 +22,9 @@
 SPAD = 80
 CPAD = 48
 EARLY = 512
-ROWS = EARLY + 4 * CPAD
-SLOTS = tuple(WIN + k * SPAD for k in range(4)) + (EARLY, EARLY + 2 * CPAD)
+LATE = 128
+ROWS = EARLY + 2 * LATE
+SLOTS = tuple(WIN + k * SPAD for k in range(4)) + (EARLY, EARLY + CPAD)
 BIAS_ROWS = 759
 LOG2E = 1.4426950408889634
 SCALE = LOG2E * HEAD_DIM ** (-0.5)
@@ -73,10 +74,10 @@
         side = 0 if row < HH else 1
         h = row if row < HH else row - HH - WH
         if col < HW:
-            return cw + side * CPAD + (z * HH + h) * HW + col
+            return cw + side * LATE + (z * HH + h) * HW + col
         if col < HW + WW:
             return (n, s)[side] + (z * HH + h) * WW + col - HW
-        return ce + side * CPAD + (z * HH + h) * HW + col - HW - WW
+        return ce + side * LATE + (z * HH + h) * HW + col - HW - WW
 
     keys = []
     query_token = []
@@ -158,13 +159,14 @@
     counter = [0]
     sent = []
 
-    def send(source, target, device):
+    def send(source, target, device, begin=True):
         copy = pltpu.make_async_remote_copy(
             src_ref=source, dst_ref=target, send_sem=send_sem.at[counter[0]], recv_sem=recv_sem.at[counter[0]],
             device_id=device, device_id_type=MESH,
         )
         counter[0] += 1
-        copy.start()
+        if begin:
+            copy.start()
         sent.append(copy)
         return copy
 
@@ -374,82 +376,105 @@
     to_west = send(strip_out.at[pl.ds(2 * SPAD, SPAD)], slot(3), west)
     to_east = send(strip_out.at[pl.ds(3 * SPAD, SPAD)], slot(2), east)
 
-    start_weights(3)
     xq[...] = jnp.dot(query_ref[...], rows[0:WIN], preferred_element_type=F32).astype(BF16)
     rows[SLOTS[3] + SPAD : EARLY] = jnp.zeros((EARLY - SLOTS[3] - SPAD, D), BF16)
+    for side in range(2):
+        first = EARLY + side * LATE
+        rows[first + 2 * CPAD : first + LATE] = jnp.zeros((LATE - 2 * CPAD, D), BF16)
     pass_across(2)
     bias_rows1(6, 7)
     finish_weights(2)
-    pass_first(3)
-    bias_rows1(13, 5)
+    start_weights(3)
 
     @pl.loop(0, 2)
     def _(t):
         lanes = pl.ds(pl.multiple_of(t * 256, 256), 256)
         q1[:, lanes] = jnp.dot(xq[...], wq[1, :, lanes], preferred_element_type=F32)
 
-    corner_copies = []
-    for side, arrived in ((0, to_south), (1, to_north)):
-        arrived.wait_recv()
+    arrivals = (to_south, to_north)
+    corner_copies = [
+        [
+            send(
+                corner_out.at[pl.ds((side * 2 + n) * CPAD, CPAD)], rows.at[pl.ds(start + side * LATE, CPAD)], device, False
+            )
+            for n, (start, device) in enumerate(((SLOTS[5], west), (SLOTS[4], east)))
+        ]
+        for side in range(2)
+    ]
+
+    def forward(side):
+        arrivals[side].wait_recv()
         strip = rows[SLOTS[side] : SLOTS[side] + SPAD]
         pieces = jnp.dot(corner_ref[...], strip, preferred_element_type=F32).astype(BF16)
-        first = side * 2 * CPAD
-        corner_out[first : first + 2 * CPAD] = pieces
-        for n, (start, device) in enumerate(((SLOTS[5], west), (SLOTS[4], east))):
-            corner_copies.append(send(
-                corner_out.at[pl.ds(first + n * CPAD, CPAD)], rows.at[pl.ds(start + side * CPAD, CPAD)], device
-            ))
+        corner_out[side * 2 * CPAD : (side * 2 + 2) * CPAD] = pieces
+        for copy in corner_copies[side]:
+            copy.start()
+
+    def corners_in(side):
+        for copy in corner_copies[side]:
+            copy.wait_recv()
+
+    south_first = y == 0
+
+    def by_side(action, turn):
+        @pl.when(south_first)
+        def _():
+            action(1 - turn)
+
+        @pl.when(jnp.logical_not(south_first))
+        def _():
+            action(turn)
+
+    by_side(forward, 0)
+    bias_rows1(13, 7)
+    pass_first(3)
+    by_side(forward, 1)
+    to_west.wait_recv()
+    to_east.wait_recv()
+
+    def attend1(g, w):
+        lanes = slice(g * 128, g * 128 + 128)
+        span = pl.ds(pl.multiple_of(w * QPAD, 8), QPAD)
+        keys = pl.ds(pl.multiple_of(w * WIN, 16), WIN)
+        q = q1[span, lanes]
+        k = kv1[keys, lanes]
+        v = kv1[keys, D + g * 128 : D + g * 128 + 128]
+        v_ones = jnp.concatenate([v, jnp.ones((WIN, 128), BF16)], axis=1)
+        stacked = jnp.concatenate([jnp.where(lane_head == u, q, 0.0) for u in range(4)], axis=0).astype(BF16)
+        scores = lax.dot_general(stacked, k, (((1,), (1,)), ((), ())), preferred_element_type=F32)
+        bias = bias1[w, g * 4 : g * 4 + 4, :, :WIN].reshape(4 * QPAD, WIN)
+        scores = scores * SCALE + bias
+        peak = jnp.max(scores, axis=1, keepdims=True)
+        weight = jnp.exp2(scores - peak).astype(BF16)
+        both = jnp.dot(weight, v_ones, preferred_element_type=F32)
+        top, bottom = both[:QPAD, :128], both[:QPAD, 128:]
+        for u in range(1, 4):
+            mine = lane_head == u
+            top = jnp.where(mine, both[u * QPAD : u * QPAD + QPAD, :128], top)
+            bottom = jnp.where(mine, both[u * QPAD : u * QPAD + QPAD, 128:], bottom)
+        mixed1[span, lanes] = top / bottom
+
+    def window_pair(turn):
+        side = jnp.where(south_first, 1 - turn, turn)
+        spans = [pl.ds(pl.multiple_of((side * 2 + b) * WIN, 16), WIN) for b in range(2)]
+        for span in spans:
+            xk[span] = jnp.dot(key_ref[span, :EARLY], rows[:EARLY], preferred_element_type=F32).astype(BF16)
+        by_side(corners_in, turn)
+        late = pl.ds(pl.multiple_of(EARLY + side * LATE, 128), LATE)
+        for span in spans:
+            xk[span] += jnp.dot(key_ref[span, late], rows[late], preferred_element_type=F32).astype(BF16)
+        pair = pl.ds(pl.multiple_of(side * 2 * WIN, 16), 2 * WIN)
+        for t in range(4):
+            lanes = slice(t * 256, t * 256 + 256)
+            kv1[pair, lanes] = jnp.dot(xk[pair], wq[1, :, D + t * 256 : D + t * 256 + 256], preferred_element_type=F32).astype(BF16)
+        for g in range(4):
+            for b in range(2):
+                attend1(g, side * 2 + b)
+
+    window_pair(0)
     pass_second(3)
     pass_across(3)
-    bias_rows1(18, 2)
-    to_west.wait_recv()
-    to_east.wait_recv()
-
-    @pl.loop(0, 4)
-    def _(t):
-        span = pl.ds(pl.multiple_of(t * WIN, 16), WIN)
-        xk[span] = jnp.dot(key_ref[span, :EARLY], rows[:EARLY], preferred_element_type=F32).astype(BF16)
-
-    for copy in corner_copies:
-        copy.wait_recv()
-
-    @pl.loop(0, 4)
-    def _(t):
-        span = pl.ds(pl.multiple_of(t * WIN, 16), WIN)
-        xk[span] += jnp.dot(key_ref[span, EARLY:], rows[EARLY:], preferred_element_type=F32).astype(BF16)
-
-    @pl.loop(0, 4)
-    def _(t):
-        lanes = pl.ds(pl.multiple_of(t * 256, 256), 256)
-        source = pl.ds(pl.multiple_of(D + t * 256, 256), 256)
-        kv1[:, lanes] = jnp.dot(xk[...], wq[1, :, source], preferred_element_type=F32).astype(BF16)
-
-    def attend1(g):
-        lanes = slice(g * 128, g * 128 + 128)
-        for w in range(4):
-            span = slice(w * QPAD, w * QPAD + QPAD)
-            keys = slice(w * WIN, w * WIN + WIN)
-            q = q1[span, lanes]
-            k = kv1[keys, lanes]
-            v = kv1[keys, D + g * 128 : D + g * 128 + 128]
-            v_ones = jnp.concatenate([v, jnp.ones((WIN, 128), BF16)], axis=1)
-            stacked = jnp.concatenate([jnp.where(lane_head == u, q, 0.0) for u in range(4)], axis=0).astype(BF16)
-            scores = lax.dot_general(stacked, k, (((1,), (1,)), ((), ())), preferred_element_type=F32)
-            bias = bias1[w, g * 4 : g * 4 + 4, :, :WIN].reshape(4 * QPAD, WIN)
-            scores = scores * SCALE + bias
-            peak = jnp.max(scores, axis=1, keepdims=True)
-            weight = jnp.exp2(scores - peak).astype(BF16)
-            both = jnp.dot(weight, v_ones, preferred_element_type=F32)
-            top, bottom = both[:QPAD, :128], both[:QPAD, 128:]
-            for u in range(1, 4):
-                mine = lane_head == u
-                top = jnp.where(mine, both[u * QPAD : u * QPAD + QPAD, :128], top)
-                bottom = jnp.where(mine, both[u * QPAD : u * QPAD + QPAD, 128:], bottom)
-            mixed1[span, lanes] = top / bottom
-
-    for g in range(4):
-        attend1(g)
-
+    window_pair(1)
     finish_weights(3)
     natural = jnp.dot(back_ref[...], mixed1[...].astype(BF16), preferred_element_type=F32).astype(BF16)
     projected = jnp.dot(natural, wo[1], preferred_element_type=F32)

time: 61.5 us -> 62.8 us (1.021)
  Pallas kernels: 59.6 us -> 60.9 us
    pallas_call x1, Pallas kernels: 59.6 us -> 60.9 us  [local(): pl.pallas_call(functools.partial(kernel, lat_count=lat_count, lon_count=l...]
where the time goes in v6:
time: 62.8 us; the launch traced here: 62.6 us
  Pallas kernels  60.9 us (97%)
  local copies, waits for them, and re-layouts  1.67 us (3%)
    pallas_call x1, Pallas kernels, local(): pl.pallas_call(functools.partial(kernel, lat_count=lat_count, lon_count=l...  60.9 us
    unnamed x1, local copies, waits for them, and re-layouts  1.67 us

profile of v6, /device:TPU:1, one launch (start us, length us, event | category | flops | bytes accessed | tf_op | source)
XLA Modules:
  0.0 62.6 jit_solution(13393774226356052561)
XLA Ops:
  0.0 60.9 %two_blocks.1 = bf16[72,2,512]{2,1,0:T(2,128)(2,1)} custom-call(bf16[72,2,512]{2,1,0:T(2,128)(2,1)} %bitcast.9, f32[2,512]{1,0:T(2,128)} %gain_hbm.1, bf16[2,64,1536]{2,1,0:T(8,128)(2,1)} %qkv_ref.1, bf16[2,64,512]{2,1,0:T(8,128)(2,1)} %outw_ref.1, f32[2,16,759]{2,1,0:T(8,128)} %bitcast.10, s32[144,144]{1,0:T(8,128)} %idx_hbm.1, s32[6,2,12]{2,1,0:T(2,128)} %bitcast.11, ...), custom_call_target="tpu_custom_call" | custom-call | tf_op jit(solution)/shard_map/two_blocks/pallas_call | solution.py:497
  60.9 1.7 %copy.16 = bf16[1,2,6,12,512]{4,1,3,2,0:T(2,128)(2,1)} copy(bf16[1,2,6,12,512]{4,1,3,2,0:T(2,128)(2,1)} %bitcast.8) | data formatting | bytes 294912

commit v7 on v6

--- a/solution.py
+++ b/solution.py
@@ -323,6 +323,7 @@
         lanes = slice(t * 256, t * 256 + 256)
         partial[:, lanes] = chip_product(0, lanes) + chip_product(1, lanes) + chip_product(3, lanes)
     pass_across(0)
+    bias_rows1(6, 4)
     stages[0][9].wait_recv()
 
     for t in range(6):
@@ -382,7 +383,7 @@
         first = EARLY + side * LATE
         rows[first + 2 * CPAD : first + LATE] = jnp.zeros((LATE - 2 * CPAD, D), BF16)
     pass_across(2)
-    bias_rows1(6, 7)
+    bias_rows1(10, 5)
     finish_weights(2)
     start_weights(3)
 
@@ -426,7 +427,7 @@
             action(turn)
 
     by_side(forward, 0)
-    bias_rows1(13, 7)
+    bias_rows1(15, 5)
     pass_first(3)
     by_side(forward, 1)
     to_west.wait_recv()

time: 62.8 us -> 61.6 us (0.981)
  Pallas kernels: 60.9 us -> 59.7 us
    pallas_call x1, Pallas kernels: 60.9 us -> 59.7 us  [local(): pl.pallas_call(functools.partial(kernel, lat_count=lat_count, lon_count=l...]
where the time goes in v7:
time: 61.6 us; the launch traced here: 61.4 us
  Pallas kernels  59.7 us (97%)
  local copies, waits for them, and re-layouts  1.67 us (3%)
    pallas_call x1, Pallas kernels, local(): pl.pallas_call(functools.partial(kernel, lat_count=lat_count, lon_count=l...  59.7 us
    unnamed x1, local copies, waits for them, and re-layouts  1.67 us

profile of v7, /device:TPU:1, one launch (start us, length us, event | category | flops | bytes accessed | tf_op | source)
XLA Modules:
  0.0 61.4 jit_solution(10017028006563381897)
XLA Ops:
  0.0 59.7 %two_blocks.1 = bf16[72,2,512]{2,1,0:T(2,128)(2,1)} custom-call(bf16[72,2,512]{2,1,0:T(2,128)(2,1)} %bitcast.9, f32[2,512]{1,0:T(2,128)} %gain_hbm.1, bf16[2,64,1536]{2,1,0:T(8,128)(2,1)} %qkv_ref.1, bf16[2,64,512]{2,1,0:T(8,128)(2,1)} %outw_ref.1, f32[2,16,759]{2,1,0:T(8,128)} %bitcast.10, s32[144,144]{1,0:T(8,128)} %idx_hbm.1, s32[6,2,12]{2,1,0:T(2,128)} %bitcast.11, ...), custom_call_target="tpu_custom_call" | custom-call | tf_op jit(solution)/shard_map/two_blocks/pallas_call | solution.py:498
  59.7 1.7 %copy.16 = bf16[1,2,6,12,512]{4,1,3,2,0:T(2,128)(2,1)} copy(bf16[1,2,6,12,512]{4,1,3,2,0:T(2,128)(2,1)} %bitcast.8) | data formatting | bytes 294912
